TPU v7x, 32 devices: a whole 2x2x4 slice. The times are simulated.
32 devices in a mesh: tm: 4 (over x, core), space: 8 (over z, y).
Axes of the slice: x: 2, y: 2, z: 4, core: 2. Of those that a mesh axis runs over, the one named last changes fastest.
Arguments:
- snapshots: bfloat16 [1008, 5, 16, 8, 128], P('tm', None, 'space'), may hold values from -6 to 6
- picks: int32 [896], P('tm'), may hold values from 0 to 251, as said below
- basis: bfloat16 [32, 5, 16, 8, 128], P(None, None, 'space'), may hold values from -0.0390625 to 0.0390625
- kappa: float32 [5, 16, 8, 128], P(None, 'space'), may hold values from 0.03 to 0.16
Outputs:
- coefficients: float32 [896, 32], P('tm')
- factor: float32 [561, 561], replicated
Inputs may be any that keep to these rules, and one draw needn't show every extreme that they name: `picks`: within each time group's 224 consecutive entries the indices are distinct, and 0 and 251 both occur.
All inputs are finite; a program needn't handle non-finite values.
Results may differ from a plain program's by a relative error of at most 0.0003.
Values may be sent and summed in bfloat16 or wider, within the bound.
A program may use at most 64 MiB of HBM per device.

v0:
```python
import functools

import jax
import jax.numpy as jnp
import numpy as np
from jax import lax
from jax.experimental import pallas as pl
from jax.experimental.pallas import tpu as pltpu
from jax.sharding import PartitionSpec as P

MESH = pl.DeviceIdType.MESH
HIGHEST = lax.Precision.HIGHEST
NT = (((1,), (1,)), ((), ()))
TN = (((0,), (0,)), ((), ()))
CHUNK = 64
F32 = jnp.float32
BF16 = jnp.bfloat16


def project_kernel(count, s_ref, b_ref, k_ref, low_ref, high_ref, picks_ref, out_ref, g_ref, acc_ref):
    step = pl.program_id(0)
    modes, nv, nx, ny, nz = b_ref.shape
    wide = modes * ny

    @pl.when(step == 0)
    def _():
        acc_ref[...] = jnp.zeros_like(acc_ref)
        yi = lax.broadcasted_iota(jnp.int32, (wide, nz), 0) % ny
        zi = lax.broadcasted_iota(jnp.int32, (wide, nz), 1)

        def spread(plane):
            return jnp.broadcast_to(plane[None], (modes, ny, nz)).reshape(wide, nz)

        for v in range(nv):
            b = [b_ref[:, v, x].astype(F32).reshape(wide, nz) for x in range(nx)]
            kap = [spread(k_ref[v, x]) for x in range(nx)]
            w = [b[x] * kap[x] for x in range(nx)]
            sides = []
            for ref in (low_ref, high_ref):
                kn = ref[modes, v].astype(F32) + ref[modes + 1, v].astype(F32) + ref[modes + 2, v].astype(F32)
                sides.append(ref[:modes, v].astype(F32).reshape(wide, nz) * spread(kn))
            for x in range(nx):
                beside = (w[x - 1] if x > 0 else sides[0]) + (w[x + 1] if x < nx - 1 else sides[1])
                beside = beside + jnp.where(yi < ny - 1, pltpu.roll(w[x], wide - 1, 0), 0.0)
                beside = beside + jnp.where(yi > 0, pltpu.roll(w[x], 1, 0), 0.0)
                beside = beside + jnp.where(zi < nz - 1, pltpu.roll(w[x], nz - 1, 1), 0.0)
                beside = beside + jnp.where(zi > 0, pltpu.roll(w[x], 1, 1), 0.0)
                g = b[x] * (1.0 - 6.0 * kap[x]) + beside
                hi = g.astype(BF16)
                lo = (g - hi.astype(F32)).astype(BF16)
                at = pl.ds((v * nx + x) * nz, nz)
                g_ref[pl.ds(0, wide), at] = hi
                g_ref[pl.ds(wide, wide), at] = lo

    rows = jnp.concatenate(
        [s_ref[:, v, x].reshape(CHUNK * ny, nz) for v in range(nv) for x in range(nx)], axis=1
    )
    both = lax.dot_general(rows, g_ref[...], NT, preferred_element_type=F32)
    prod = both[:, :wide] + both[:, wide:]
    yr = lax.broadcasted_iota(jnp.int32, prod.shape, 0) % ny
    yc = lax.broadcasted_iota(jnp.int32, prod.shape, 1) % ny
    z = jnp.sum(jnp.where(yr == yc, prod, 0.0).reshape(CHUNK, ny, wide), axis=1)
    at = lax.broadcasted_iota(jnp.int32, z.shape, 0) + step * CHUNK
    z = jnp.where(at < count, z, 0.0)
    fold = (
        lax.broadcasted_iota(jnp.int32, (modes, wide), 1) // ny
        == lax.broadcasted_iota(jnp.int32, (modes, wide), 0)
    ).astype(F32)
    part = lax.dot_general(fold, z, NT, precision=HIGHEST, preferred_element_type=F32)
    lanes = acc_ref.shape[1]
    hot = (
        lax.broadcasted_iota(jnp.int32, (CHUNK, lanes), 0) + step * CHUNK
        == jnp.broadcast_to(picks_ref[...], (CHUNK, lanes))
    ).astype(F32)
    acc_ref[...] += jnp.dot(part, hot, precision=HIGHEST, preferred_element_type=F32)

    @pl.when(step == pl.num_programs(0) - 1)
    def _():
        halves = lanes // 128
        for i in range(modes // 8):
            for h in range(halves):
                out_ref[i * halves + h] = acc_ref[pl.ds(8 * i, 8), pl.ds(128 * h, 128)]


def project(snapshots, basis, kappa, low, high, picks_row):
    count, nv, nx, ny, nz = snapshots.shape
    modes = basis.shape[0]
    lanes = picks_row.shape[1]
    chunks = (modes // 8) * (lanes // 128)
    whole = lambda a: pl.BlockSpec(a.shape, lambda i: (0,) * a.ndim)
    return pl.pallas_call(
        functools.partial(project_kernel, count),
        grid=(-(-count // CHUNK),),
        out_shape=jax.ShapeDtypeStruct((chunks, 8, 128), F32),
        in_specs=[
            pl.BlockSpec((CHUNK, nv, nx, ny, nz), lambda i: (i, 0, 0, 0, 0)),
            whole(basis), whole(kappa), whole(low), whole(high), whole(picks_row),
        ],
        out_specs=pl.BlockSpec((chunks, 8, 128), lambda i: (0, 0, 0)),
        scratch_shapes=[
            pltpu.VMEM((2 * modes * ny, nv * nx * nz), BF16),
            pltpu.VMEM((modes, lanes), F32),
        ],
        compiler_params=pltpu.CompilerParams(vmem_limit_bytes=48 * 2**20),
        name="project",
    )(snapshots, basis, kappa, low, high, picks_row)


def share_kernel(n_tm, n_space, own_ref, all_ref, land_ref, send1, recv1, send2, recv2):
    chunks = own_ref.shape[0]
    tm = lax.axis_index("tm")
    sp = lax.axis_index("space")
    me = tm * n_space + sp
    total = n_tm * n_space

    def peer(i):
        other = lax.rem(me + i, total)
        return other // n_space, lax.rem(other, n_space)

    barrier = pltpu.get_barrier_semaphore()

    def greet(i, carry):
        pl.semaphore_signal(barrier, inc=1, device_id=peer(i), device_id_type=MESH)
        return carry

    lax.fori_loop(1, total, greet, 0)
    pl.semaphore_wait(barrier, total - 1)

    def part_to(owner):
        return pltpu.make_async_remote_copy(
            src_ref=own_ref.at[owner], dst_ref=land_ref.at[sp],
            send_sem=send1.at[owner], recv_sem=recv1.at[sp],
            device_id=(tm, owner), device_id_type=MESH,
        )

    def part_from(source):
        return pltpu.make_async_remote_copy(
            src_ref=own_ref.at[0], dst_ref=land_ref.at[source],
            send_sem=send1.at[0], recv_sem=recv1.at[source],
            device_id=(tm, source), device_id_type=MESH,
        )

    for owner in range(chunks):
        @pl.when(sp != owner)
        def _():
            part_to(owner).start()

    @pl.when(sp < chunks)
    def _():
        land_ref[sp] = own_ref[sp]
        for source in range(n_space):
            @pl.when(sp != source)
            def _():
                part_from(source).wait_recv()
        total_sum = land_ref[0]
        for source in range(1, n_space):
            total_sum = total_sum + land_ref[source]
        all_ref[tm, sp] = total_sum

        def give(i, carry):
            pltpu.make_async_remote_copy(
                src_ref=all_ref.at[tm, sp], dst_ref=all_ref.at[tm, sp],
                send_sem=send2.at[i], recv_sem=recv2.at[tm * chunks + sp],
                device_id=peer(i), device_id_type=MESH,
            ).start()
            return carry

        lax.fori_loop(1, total, give, 0)

    for owner in range(chunks):
        @pl.when(sp != owner)
        def _():
            part_to(owner).wait_send()

    for group in range(n_tm):
        for owner in range(chunks):
            @pl.when(jnp.logical_or(tm != group, sp != owner))
            def _():
                pltpu.make_async_remote_copy(
                    src_ref=all_ref.at[group, owner], dst_ref=all_ref.at[group, owner],
                    send_sem=send2.at[0], recv_sem=recv2.at[group * chunks + owner],
                    device_id=(group, owner), device_id_type=MESH,
                ).wait_recv()

    @pl.when(sp < chunks)
    def _():
        def done(i, carry):
            pltpu.make_async_remote_copy(
                src_ref=all_ref.at[tm, sp], dst_ref=all_ref.at[tm, sp],
                send_sem=send2.at[i], recv_sem=recv2.at[tm * chunks + sp],
                device_id=peer(i), device_id_type=MESH,
            ).wait_send()
            return carry

        lax.fori_loop(1, total, done, 0)


def share(own, n_tm, n_space):
    chunks = own.shape[0]
    total = n_tm * n_space
    return pl.pallas_call(
        functools.partial(share_kernel, n_tm, n_space),
        out_shape=jax.ShapeDtypeStruct((n_tm, chunks, 8, 128), F32),
        in_specs=[pl.BlockSpec(memory_space=pltpu.VMEM)],
        out_specs=pl.BlockSpec(memory_space=pltpu.VMEM),
        scratch_shapes=[
            pltpu.VMEM((n_space, 8, 128), F32),
            pltpu.SemaphoreType.DMA((chunks,)),
            pltpu.SemaphoreType.DMA((n_space,)),
            pltpu.SemaphoreType.DMA((total,)),
            pltpu.SemaphoreType.DMA((n_tm * chunks,)),
        ],
        compiler_params=pltpu.CompilerParams(collective_id=0, has_side_effects=True),
        name="share",
    )(own)


def eliminate(a, b):
    tiles = len(a)
    sub = lax.broadcasted_iota(jnp.int32, (8, 128), 0)
    row_of = lambda x, k: jnp.broadcast_to(x[k : k + 1, :], (8, 128))
    column_of = lambda x, k: jnp.broadcast_to(x[:, k : k + 1], (8, 128))
    diag = []
    for s in range(tiles):
        cols = [column_of(a[s], 8 * s + k) for k in range(8)]
        inv, known, a_rows, b_rows = [], [], [], []
        d = jnp.ones((8, 128), F32)
        for k in range(8):
            pivot = row_of(cols[k], k)
            d = jnp.where(sub == k, pivot, d)
            r = 1.0 / pivot
            m = jnp.where(sub > k, cols[k] * r, 0.0)
            seen = {}
            for q in range(k + 1, 8):
                seen[q] = row_of(cols[q], k)
                cols[q] = cols[q] - m * seen[q]
            a_rows.append(row_of(a[s], k))
            a[s] = a[s] - m * a_rows[k]
            if b is not None:
                b_rows.append(row_of(b[s], k))
                b[s] = b[s] - m * b_rows[k]
            inv.append(r)
            known.append(seen)
        diag.append(d)
        for i in range(s + 1, tiles):
            cols = [column_of(a[i], 8 * s + k) for k in range(8)]
            for k in range(8):
                m = cols[k] * inv[k]
                for q in range(k + 1, 8):
                    cols[q] = cols[q] - m * known[k][q]
                a[i] = a[i] - m * a_rows[k]
                if b is not None:
                    b[i] = b[i] - m * b_rows[k]
    scale = []
    for d in diag:
        y = lax.rsqrt(d)
        scale.append(y * (1.5 - 0.5 * d * y * y))
    return a, b, scale


def factor_kernel(count, n_feat, all_ref, s1_ref, s2_ref, c_ref, o_ref, f_ref, a_ref, u_ref, l_ref):
    n_tm, chunks = all_ref.shape[:2]
    padded = s1_ref.shape[0]
    blocks = padded // 128
    halves = -(-count // 128)
    lanes = halves * 128
    groups = chunks // halves
    modes = 8 * groups
    tm = lax.axis_index("tm")

    def coeffs(g):
        return jnp.concatenate(
            [
                jnp.concatenate([all_ref[g, i * halves + h] for h in range(halves)], axis=1)
                for i in range(groups)
            ],
            axis=0,
        )

    c_ref[...] = jnp.transpose(coeffs(tm))[:count, :]
    lane = lax.broadcasted_iota(jnp.int32, (modes, lanes), 1)
    top = lax.broadcasted_iota(jnp.int32, (modes, lanes), 0)
    ones = jnp.where(jnp.logical_and(lane < count, top == 0), 1.0, 0.0).astype(BF16)
    for g in range(n_tm):
        c = coeffs(g)
        hi = c.astype(BF16)
        rest = c - hi.astype(F32)
        mid = rest.astype(BF16)
        low = (rest - mid.astype(F32)).astype(BF16)
        stack = jnp.concatenate([hi, mid, low, ones], axis=0)
        f1 = jnp.dot(s1_ref[...], stack, preferred_element_type=F32)
        f2 = jnp.dot(s2_ref[...], stack, preferred_element_type=F32)
        f_ref[:, pl.ds(g * lanes, lanes)] = f1 * f2

    share_of = 1.0 / (count * n_tm)
    for j in range(blocks):
        gram = lax.dot_general(
            f_ref[pl.ds(j * 128, 128), :], f_ref[pl.ds(j * 128, padded - j * 128), :], NT,
            precision=HIGHEST, preferred_element_type=F32,
        )
        a_ref[pl.ds(j * 128, 128), pl.ds(j * 128, padded - j * 128)] = gram * share_of

    last = (blocks - 1) * 128
    ri = lax.broadcasted_iota(jnp.int32, (128, 128), 0)
    ci = lax.broadcasted_iota(jnp.int32, (128, 128), 1)
    corner = a_ref[pl.ds(last, 128), pl.ds(last, 128)]
    a_ref[pl.ds(last, 128), pl.ds(last, 128)] = corner + jnp.where(
        jnp.logical_and(ri == ci, ri + last >= n_feat), 1.0, 0.0
    )

    lane8 = lax.broadcasted_iota(jnp.int32, (8, 128), 1)
    sub8 = lax.broadcasted_iota(jnp.int32, (8, 128), 0)

    def block(j, carry):
        start = pl.multiple_of(j * 128, 128)
        a = [a_ref[pl.ds(start + 8 * i, 8), pl.ds(start, 128)] for i in range(16)]
        b = [jnp.where(lane8 == sub8 + 8 * i, 1.0, 0.0) for i in range(16)]
        a, b, scale = eliminate(a, b)
        for i in range(16):
            u_ref[pl.ds(8 * i, 8), :] = jnp.where(lane8 >= sub8 + 8 * i, a[i] * scale[i], 0.0)
            l_ref[pl.ds(8 * i, 8), :] = b[i] * scale[i]

        for jj in range(blocks - 1):
            @pl.when(j == jj)
            def _():
                here, after = jj * 128, (jj + 1) * 128
                if jj > 0:
                    o_ref[pl.ds(here, 128), pl.ds(0, here)] = jnp.zeros((128, here), F32)
                o_ref[pl.ds(here, 128), pl.ds(here, 128)] = u_ref[...]
                w = jnp.dot(
                    l_ref[...], a_ref[pl.ds(here, 128), pl.ds(after, padded - after)],
                    precision=HIGHEST, preferred_element_type=F32,
                )
                o_ref[pl.ds(here, 128), pl.ds(after, n_feat - after)] = w[:, : n_feat - after]
                for i in range(jj + 1, blocks):
                    row = i * 128
                    a_ref[pl.ds(row, 128), pl.ds(row, padded - row)] -= lax.dot_general(
                        w[:, row - after : row - after + 128], w[:, row - after :], TN,
                        precision=HIGHEST, preferred_element_type=F32,
                    )
        return carry

    lax.fori_loop(0, blocks - 1, block, 0)
    left = n_feat - last
    tiles = -(-left // 8)
    a = [a_ref[pl.ds(last + 8 * i, 8), pl.ds(last, 128)] for i in range(tiles)]
    a, _, scale = eliminate(a, None)
    for i in range(tiles):
        u_ref[pl.ds(8 * i, 8), :] = jnp.where(lane8 >= sub8 + 8 * i, a[i] * scale[i], 0.0)
    o_ref[pl.ds(last, left), pl.ds(0, last)] = jnp.zeros((left, last), F32)
    o_ref[pl.ds(last, left), pl.ds(last, left)] = u_ref[pl.ds(0, left), pl.ds(0, left)]


def selections(modes):
    first, second = np.triu_indices(modes)
    n_feat = 1 + modes + len(first)
    padded = -(-n_feat // 128) * 128
    one = 3 * modes
    s1 = np.zeros((padded, 4 * modes), np.float32)
    s2 = np.zeros((padded, 4 * modes), np.float32)
    s1[0, one] = s2[0, one] = 1.0
    for part in range(3):
        for m in range(modes):
            s1[1 + m, part * modes + m] = 1.0
        s1[1 + modes + np.arange(len(first)), part * modes + first] = 1.0
        s2[1 + modes + np.arange(len(first)), part * modes + second] = 1.0
    s2[1 : 1 + modes, one] = 1.0
    return n_feat, padded, s1, s2


def factorize(shared, count, modes):
    n_tm = shared.shape[0]
    n_feat, padded, s1, s2 = selections(modes)
    lanes = -(-count // 128) * 128
    vmem = pl.BlockSpec(memory_space=pltpu.VMEM)
    return pl.pallas_call(
        functools.partial(factor_kernel, count, n_feat),
        out_shape=(
            jax.ShapeDtypeStruct((count, modes), F32),
            jax.ShapeDtypeStruct((n_feat, n_feat), F32),
        ),
        in_specs=[vmem] * 3,
        out_specs=(vmem, vmem),
        scratch_shapes=[
            pltpu.VMEM((padded, n_tm * lanes), F32),
            pltpu.VMEM((padded, padded), F32),
            pltpu.VMEM((128, 128), F32),
            pltpu.VMEM((128, 128), F32),
        ],
        compiler_params=pltpu.CompilerParams(vmem_limit_bytes=48 * 2**20),
        name="factorize",
    )(shared, jnp.asarray(s1, BF16), jnp.asarray(s2, BF16))


def body(snapshots, picks, basis, kappa):
    n_tm, n_space = lax.axis_size("tm"), lax.axis_size("space")
    modes, count = basis.shape[0], picks.shape[0]
    hi = lax.reduce_precision(kappa, 8, 7)
    mid = lax.reduce_precision(kappa - hi, 8, 7)
    low = kappa - hi - mid
    parts = jnp.stack([hi, mid, low]).astype(BF16)

    def plane(x):
        return jnp.concatenate([basis[:, :, x], parts[:, :, x]], axis=0)

    forward = [(i, i + 1) for i in range(n_space - 1)]
    backward = [(i + 1, i) for i in range(n_space - 1)]
    from_low = lax.ppermute(plane(basis.shape[2] - 1), "space", forward)
    from_high = lax.ppermute(plane(0), "space", backward)
    lanes = -(-count // 128) * 128
    picks_row = jnp.pad(picks, (0, lanes - count), constant_values=-1).reshape(1, lanes)
    own = project(snapshots, basis, kappa, from_low, from_high, picks_row)
    shared = share(own, n_tm, n_space)
    return tuple(factorize(shared, count, modes))


def solution(mesh):
    in_specs = (
        P("tm", None, "space", None, None),
        P("tm"),
        P(None, None, "space", None, None),
        P(None, "space", None, None),
    )
    out_specs = (P("tm", None), P())
    return jax.shard_map(body, mesh=mesh, in_specs=in_specs, out_specs=out_specs, check_vma=False)
```

profile of v0, /device:TPU:0, one launch (start us, length us, event | category | flops | bytes accessed | tf_op | source)
XLA Modules:
  0.0 81.6 jit_solution(13145651191255846873)
XLA Ops:
  0.6 0.0 copy-start.3
  0.6 0.0 copy-start.4
  0.7 0.8 %fusion.2 = (bf16[1,5,2,8,128]{4,3,1,0,2:T(8,128)(2,1)S(1)}, bf16[1,5,2,8,128]{4,3,1,0,2:T(8,128)(2,1)S(1)}, bf16[1,5,2,8,128]{4,3,1,0,2:T(8,128)(2,1)S(1)}) fusion(f32[5,2,8,128]{3,2,1,0:T(8,128)} %k_ref.1), kind=kLoop, calls=%fused_computation.13 | loop fusion | flops 71680 | bytes 102400 | tf_op jit(solution)/shard_map/stack | solution.py:401
  1.5 1.1 %slice_bitcast_fusion = (bf16[32,5,8,128]{3,2,1,0:T(8,128)(2,1)S(1)}, bf16[32,5,8,128]{3,2,1,0:T(8,128)(2,1)S(1)}) fusion(bf16[32,5,2,8,128]{4,3,2,1,0:T(8,128)(2,1)} %b_ref.1), kind=kLoop, calls=%fused_computation.2 | loop fusion | bytes 1310720 | tf_op jit(solution)/shard_map/squeeze | solution.py:404
  2.7 4.9 %collective-permute-start = (bf16[35,5,8,128]{3,2,1,0:T(8,128)(2,1)S(1)}, bf16[35,5,8,128]{3,2,1,0:T(8,128)(2,1)S(1)}, u32[]{:S(2)}, u32[]{:S(2)}) collective-permute-start(bf16[35,5,8,128]{3,2,1,0:T(8,128)(2,1)S(1)} %pad_maximum_fusion), channel_id=1, source_target_pairs={{0,1},{1,2},{2,3},{3,4},{4,5},{5,6},{6,7},{8,9},{9,10},{10,11},{11... | collective-permute-start | bytes 1075208 | tf_op jit(solution)/shard_map/ppermute | solution.py:408
  7.6 1.3 %collective-permute-start.1 = (bf16[35,5,8,128]{3,2,1,0:T(8,128)(2,1)S(1)}, bf16[35,5,8,128]{3,2,1,0:T(8,128)(2,1)S(1)}, u32[]{:S(2)}, u32[]{:S(2)}) collective-permute-start(bf16[35,5,8,128]{3,2,1,0:T(8,128)(2,1)S(1)} %pad_maximum_fusion.1), channel_id=1, source_target_pairs={{1,0},{2,1},{3,2},{4,3},{5,4},{6,5},{7,6},{9,8},{10,9},{11,10},{12... | collective-permute-start | bytes 1075208 | tf_op jit(solution)/shard_map/ppermute | solution.py:409
  8.9 0.7 pad.4
  9.6 13.2 %collective-permute-done.low_ref = bf16[35,5,8,128]{3,2,1,0:T(8,128)(2,1)S(1)} collective-permute-done((bf16[35,5,8,128]{3,2,1,0:T(8,128)(2,1)S(1)}, bf16[35,5,8,128]{3,2,1,0:T(8,128)(2,1)S(1)}, u32[]{:S(2)}, u32[]{:S(2)}) %collective-permute-start) | collective-permute-done | bytes 358432 | tf_op jit(solution)/shard_map/ppermute | solution.py:408
  22.9 0.0 collective-permute-done.1.high_ref
  22.9 0.0 copy-start
  22.9 1.1 %copy-done = bf16[32,5,2,8,128]{4,3,2,1,0:T(8,128)(2,1)S(1)} copy-done((bf16[32,5,2,8,128]{4,3,2,1,0:T(8,128)(2,1)S(1)}, bf16[32,5,2,8,128]{4,3,2,1,0:T(8,128)(2,1)}, u32[]{:S(2)}) %copy-start) | copy-done | bytes 655384
  24.0 0.0 copy-start.2
  24.0 0.8 copy-done.2
  24.7 8.0 %project.1.own_ref = f32[8,8,128]{2,1,0:T(8,128)S(1)} custom-call(bf16[252,5,2,8,128]{4,3,2,1,0:T(8,128)(2,1)} %s_ref.1, bf16[32,5,2,8,128]{4,3,2,1,0:T(8,128)(2,1)S(1)} %copy-done, f32[5,2,8,128]{3,2,1,0:T(8,128)S(1)} %copy-done.2, bf16[35,5,8,128]{3,2,1,0:T(8,128)(2,1)S(1)} %collective-permute-done.low_ref, ...), custom_call_target="tpu_custom_call" | custom-call | tf_op jit(solution)/shard_map/project/pallas_call | solution.py:91
  32.7 0.0 copy-start.5
  32.8 0.6 copy-done.5
  33.4 17.7 %share.1.all_ref = f32[4,8,8,128]{3,2,1,0:T(8,128)} custom-call(f32[8,8,128]{2,1,0:T(8,128)} %copy-done.5), custom_call_target="tpu_custom_call" | custom-call | tf_op jit(solution)/shard_map/share/pallas_call | solution.py:201
  51.0 0.0 copy-done.3
  51.0 0.0 copy-done.4
  51.0 0.0 copy-start.1
  51.1 0.9 %copy-done.1 = f32[4,8,8,128]{3,2,1,0:T(8,128)S(1)} copy-done((f32[4,8,8,128]{3,2,1,0:T(8,128)S(1)}, f32[4,8,8,128]{3,2,1,0:T(8,128)}, u32[]{:S(2)}) %copy-start.1) | copy-done | bytes 131096
  52.0 29.0 %factorize.1 = (f32[224,32]{1,0:T(8,128)S(1)}, f32[561,561]{1,0:T(8,128)}) custom-call(f32[4,8,8,128]{3,2,1,0:T(8,128)S(1)} %copy-done.1, bf16[640,128]{1,0:T(8,128)(2,1)S(1)} %copy-done.4, bf16[640,128]{1,0:T(8,128)(2,1)S(1)} %copy-done.3), custom_call_target="tpu_custom_call" | custom-call | tf_op jit(solution)/shard_map/factorize/pallas_call | solution.py:376
  80.9 0.7 copy.14
  (4 shorter events, 0.1 us)
Async XLA Ops:
  0.6 50.4 %copy-start.3 = (bf16[640,128]{1,0:T(8,128)(2,1)S(1)}, bf16[640,128]{1,0:T(8,128)(2,1)}, u32[]{:S(2)}) copy-start(bf16[640,128]{1,0:T(8,128)(2,1)} %constant.7.clone.s2_ref) | copy-start | bytes 491524
  0.6 50.4 %copy-start.4 = (bf16[640,128]{1,0:T(8,128)(2,1)S(1)}, bf16[640,128]{1,0:T(8,128)(2,1)}, u32[]{:S(2)}) copy-start(bf16[640,128]{1,0:T(8,128)(2,1)} %constant.6.clone.s1_ref) | copy-start | bytes 491524
  2.7 20.2 %collective-permute-start = (bf16[35,5,8,128]{3,2,1,0:T(8,128)(2,1)S(1)}, bf16[35,5,8,128]{3,2,1,0:T(8,128)(2,1)S(1)}, u32[]{:S(2)}, u32[]{:S(2)}) collective-permute-start(bf16[35,5,8,128]{3,2,1,0:T(8,128)(2,1)S(1)} %pad_maximum_fusion), channel_id=1, source_target_pairs={{0,1},{1,2},{2,3},{3,4},{4,5},{5,6},{6,7},{8,9},{9,10},{10,11},{11... | collective-permute-start | bytes 1075208 | tf_op jit(solution)/shard_map/ppermute | solution.py:408
  7.6 15.2 %collective-permute-start.1 = (bf16[35,5,8,128]{3,2,1,0:T(8,128)(2,1)S(1)}, bf16[35,5,8,128]{3,2,1,0:T(8,128)(2,1)S(1)}, u32[]{:S(2)}, u32[]{:S(2)}) collective-permute-start(bf16[35,5,8,128]{3,2,1,0:T(8,128)(2,1)S(1)} %pad_maximum_fusion.1), channel_id=1, source_target_pairs={{1,0},{2,1},{3,2},{4,3},{5,4},{6,5},{7,6},{9,8},{10,9},{11,10},{12... | collective-permute-start | bytes 1075208 | tf_op jit(solution)/shard_map/ppermute | solution.py:409
  22.9 1.1 %copy-start = (bf16[32,5,2,8,128]{4,3,2,1,0:T(8,128)(2,1)S(1)}, bf16[32,5,2,8,128]{4,3,2,1,0:T(8,128)(2,1)}, u32[]{:S(2)}) copy-start(bf16[32,5,2,8,128]{4,3,2,1,0:T(8,128)(2,1)} %b_ref.1) | copy-start | bytes 1966084
  24.0 0.8 copy-start.2
  32.7 0.6 copy-start.5
  51.0 0.9 %copy-start.1 = (f32[4,8,8,128]{3,2,1,0:T(8,128)S(1)}, f32[4,8,8,128]{3,2,1,0:T(8,128)}, u32[]{:S(2)}) copy-start(f32[4,8,8,128]{3,2,1,0:T(8,128)} %share.1.all_ref) | copy-start | bytes 393220
where the time goes:
time: 82 us; the launch traced here: 81.6 us
  Pallas kernels  54.6 us (67%)
  waiting for transfers between devices  13.2 us (16%)
  starting transfers between devices  6.19 us (8%)
  local copies, waits for them, and re-layouts  5.9 us (7%)
  other arithmetic  0.92 us (1%)
    pallas_call x1, Pallas kernels, factorize(): pl.pallas_call(functools.partial(factor_kernel, count, n_feat), out_shape...  29 us
    pallas_call x1, Pallas kernels, share(): pl.pallas_call(functools.partial(share_kernel, n_tm, n_space), out_shape=...  17.7 us
    ppermute x1, waiting for transfers between devices, body(): from_low = lax.ppermute(plane(basis.shape[2] - 1), 'space', forward)  13.2 us
    pallas_call x1, Pallas kernels, project(): pl.pallas_call(functools.partial(project_kernel, count), grid=(-(-count /...  7.99 us
    ppermute x1, starting transfers between devices, body(): from_low = lax.ppermute(plane(basis.shape[2] - 1), 'space', forward)  4.89 us
    unnamed x12, local copies, waits for them, and re-layouts  3.39 us
  transfers between devices with their start and end apart: 2, of which 1 were waited for; matrix products, arithmetic and copies ran while one was open for 1% of the time, Pallas kernels for 0%

commit v1 on v0

--- a/solution.py
+++ b/solution.py
@@ -17,133 +17,177 @@
 BF16 = jnp.bfloat16
 
 
-def project_kernel(count, s_ref, b_ref, k_ref, low_ref, high_ref, picks_ref, out_ref, g_ref, acc_ref):
-    step = pl.program_id(0)
-    modes, nv, nx, ny, nz = b_ref.shape
-    wide = modes * ny
-
-    @pl.when(step == 0)
-    def _():
-        acc_ref[...] = jnp.zeros_like(acc_ref)
-        yi = lax.broadcasted_iota(jnp.int32, (wide, nz), 0) % ny
-        zi = lax.broadcasted_iota(jnp.int32, (wide, nz), 1)
-
-        def spread(plane):
-            return jnp.broadcast_to(plane[None], (modes, ny, nz)).reshape(wide, nz)
-
+def gather_kernel(
+    n_tm, n_space, chunks, s_any, b_ref, k_ref, picks_ref, all_ref,
+    s_ref, g_ref, z_ref, hb_ref, hk_ref, own_ref, land_ref,
+    load, send_b, recv_b, send_k, recv_k, send_f, recv_f, send1, recv1, send2, recv2,
+):
+    count, nv, nx, ny, nz = s_any.shape
+    modes = b_ref.shape[0]
+    wide, half = modes * ny, modes // 2
+    lanes = picks_ref.shape[1]
+    rows_all = s_ref.shape[0]
+    tm = lax.axis_index("tm")
+    sp = lax.axis_index("space")
+    core = lax.rem(tm, 2)
+    sibling = tm + 1 - 2 * core
+    me = tm * n_space + sp
+    total = n_tm * n_space
+
+    def peer(i):
+        other = lax.rem(me + i, total)
+        return other // n_space, lax.rem(other, n_space)
+
+    loading = pltpu.make_async_copy(s_any, s_ref.at[pl.ds(0, count)], load)
+    loading.start()
+    barrier = pltpu.get_barrier_semaphore()
+
+    def greet(i, carry):
+        pl.semaphore_signal(barrier, inc=1, device_id=peer(i), device_id_type=MESH)
+        return carry
+
+    lax.fori_loop(1, total, greet, 0)
+    pl.semaphore_wait(barrier, total - 1)
+
+    def remote(src, dst, send, recv, device):
+        return pltpu.make_async_remote_copy(
+            src_ref=src, dst_ref=dst, send_sem=send, recv_sem=recv,
+            device_id=device, device_id_type=MESH,
+        )
+
+    def plane_copies(side):
+        x = nx - 1 if side == 0 else 0
+        to = lax.rem(sp + (1 if side == 0 else n_space - 1), n_space)
+        mine = pl.ds(core * half, half)
+        return (
+            remote(b_ref.at[mine, :, x], hb_ref.at[side, mine], send_b.at[side], recv_b.at[side], (tm, to)),
+            remote(k_ref.at[:, x], hk_ref.at[side], send_k.at[side], recv_k.at[side], (tm, to)),
+        )
+
+    def forward(side):
+        mine = pl.ds(core * half, half)
+        return remote(
+            hb_ref.at[side, mine], hb_ref.at[side, mine], send_f.at[side], recv_f.at[side], (sibling, sp)
+        )
+
+    sends = (sp < n_space - 1, sp > 0)
+    receives = (sp > 0, sp < n_space - 1)
+    for side in range(2):
+        @pl.when(sends[side])
+        def _():
+            for copy in plane_copies(side):
+                copy.start()
+
+        @pl.when(jnp.logical_not(receives[side]))
+        def _():
+            hb_ref[side] = jnp.zeros(hb_ref.shape[1:], BF16)
+            hk_ref[side] = jnp.zeros(hk_ref.shape[1:], F32)
+
+    def store(g, at_row, v, x):
+        size = g.shape[0]
+        hi = g.astype(BF16)
+        lo = (g - hi.astype(F32)).astype(BF16)
+        at = pl.ds((v * nx + x) * nz, nz)
+        g_ref[pl.ds(at_row, size), at] = hi
+        g_ref[pl.ds(wide + at_row, size), at] = lo
+
+    def spread(plane, many):
+        return jnp.broadcast_to(plane[None], (many, ny, nz)).reshape(many * ny, nz)
+
+    yi = lax.broadcasted_iota(jnp.int32, (wide, nz), 0) % ny
+    zi = lax.broadcasted_iota(jnp.int32, (wide, nz), 1)
+    for v in range(nv):
+        b = [b_ref[:, v, x].astype(F32).reshape(wide, nz) for x in range(nx)]
+        kap = [spread(k_ref[v, x], modes) for x in range(nx)]
+        w = [b[x] * kap[x] for x in range(nx)]
+        for x in range(nx):
+            g = b[x] * (1.0 - 6.0 * kap[x])
+            if x > 0:
+                g = g + w[x - 1]
+            if x < nx - 1:
+                g = g + w[x + 1]
+            g = g + jnp.where(yi < ny - 1, pltpu.roll(w[x], wide - 1, 0), 0.0)
+            g = g + jnp.where(yi > 0, pltpu.roll(w[x], 1, 0), 0.0)
+            g = g + jnp.where(zi < nz - 1, pltpu.roll(w[x], nz - 1, 1), 0.0)
+            g = g + jnp.where(zi > 0, pltpu.roll(w[x], 1, 1), 0.0)
+            store(g, 0, v, x)
+
+    if rows_all > count:
+        s_ref[pl.ds(count, rows_all - count)] = jnp.zeros((rows_all - count,) + s_ref.shape[1:], BF16)
+    loading.wait()
+
+    yr = lax.broadcasted_iota(jnp.int32, (CHUNK * ny, wide), 0) % ny
+    yc = lax.broadcasted_iota(jnp.int32, (CHUNK * ny, wide), 1) % ny
+
+    def contract(i):
+        at = pl.ds(i * CHUNK, CHUNK)
+        rows = jnp.concatenate(
+            [s_ref[at, v, x].reshape(CHUNK * ny, nz) for v in range(nv) for x in range(nx)], axis=1
+        )
+        both = lax.dot_general(rows, g_ref[...], NT, preferred_element_type=F32)
+        prod = both[:, :wide] + both[:, wide:]
+        return jnp.sum(jnp.where(yr == yc, prod, 0.0).reshape(CHUNK, ny, wide), axis=1)
+
+    def inner(i, carry):
+        z_ref[pl.ds(pl.multiple_of(i * CHUNK, CHUNK), CHUNK), :] = contract(i)
+        return carry
+
+    lax.fori_loop(0, rows_all // CHUNK, inner, 0)
+
+    for side in range(2):
+        @pl.when(receives[side])
+        def _():
+            for copy in plane_copies(side):
+                copy.wait_recv()
+            forward(side).start()
+
+    def outer_modes(which):
+        row = pl.multiple_of(which * (half * ny), half * ny)
         for v in range(nv):
-            b = [b_ref[:, v, x].astype(F32).reshape(wide, nz) for x in range(nx)]
-            kap = [spread(k_ref[v, x]) for x in range(nx)]
-            w = [b[x] * kap[x] for x in range(nx)]
-            sides = []
-            for ref in (low_ref, high_ref):
-                kn = ref[modes, v].astype(F32) + ref[modes + 1, v].astype(F32) + ref[modes + 2, v].astype(F32)
-                sides.append(ref[:modes, v].astype(F32).reshape(wide, nz) * spread(kn))
-            for x in range(nx):
-                beside = (w[x - 1] if x > 0 else sides[0]) + (w[x + 1] if x < nx - 1 else sides[1])
-                beside = beside + jnp.where(yi < ny - 1, pltpu.roll(w[x], wide - 1, 0), 0.0)
-                beside = beside + jnp.where(yi > 0, pltpu.roll(w[x], 1, 0), 0.0)
-                beside = beside + jnp.where(zi < nz - 1, pltpu.roll(w[x], nz - 1, 1), 0.0)
-                beside = beside + jnp.where(zi > 0, pltpu.roll(w[x], 1, 1), 0.0)
-                g = b[x] * (1.0 - 6.0 * kap[x]) + beside
-                hi = g.astype(BF16)
-                lo = (g - hi.astype(F32)).astype(BF16)
-                at = pl.ds((v * nx + x) * nz, nz)
-                g_ref[pl.ds(0, wide), at] = hi
-                g_ref[pl.ds(wide, wide), at] = lo
-
-    rows = jnp.concatenate(
-        [s_ref[:, v, x].reshape(CHUNK * ny, nz) for v in range(nv) for x in range(nx)], axis=1
-    )
-    both = lax.dot_general(rows, g_ref[...], NT, preferred_element_type=F32)
-    prod = both[:, :wide] + both[:, wide:]
-    yr = lax.broadcasted_iota(jnp.int32, prod.shape, 0) % ny
-    yc = lax.broadcasted_iota(jnp.int32, prod.shape, 1) % ny
-    z = jnp.sum(jnp.where(yr == yc, prod, 0.0).reshape(CHUNK, ny, wide), axis=1)
-    at = lax.broadcasted_iota(jnp.int32, z.shape, 0) + step * CHUNK
-    z = jnp.where(at < count, z, 0.0)
+            for side, x in ((0, 0), (1, nx - 1)):
+                plane = hb_ref[side, pl.ds(which * half, half), v].astype(F32).reshape(half * ny, nz)
+                store(plane * spread(hk_ref[side, v], half), row, v, x)
+
+    outer_modes(core)
+    for side in range(2):
+        @pl.when(receives[side])
+        def _():
+            forward(side).wait_recv()
+    outer_modes(1 - core)
+
+    def outer(i, carry):
+        z_ref[pl.ds(pl.multiple_of(i * CHUNK, CHUNK), CHUNK), :] += contract(i)
+        return carry
+
+    lax.fori_loop(0, rows_all // CHUNK, outer, 0)
+
     fold = (
         lax.broadcasted_iota(jnp.int32, (modes, wide), 1) // ny
         == lax.broadcasted_iota(jnp.int32, (modes, wide), 0)
     ).astype(F32)
-    part = lax.dot_general(fold, z, NT, precision=HIGHEST, preferred_element_type=F32)
-    lanes = acc_ref.shape[1]
+    part = lax.dot_general(fold, z_ref[...], NT, precision=HIGHEST, preferred_element_type=F32)
     hot = (
-        lax.broadcasted_iota(jnp.int32, (CHUNK, lanes), 0) + step * CHUNK
-        == jnp.broadcast_to(picks_ref[...], (CHUNK, lanes))
+        lax.broadcasted_iota(jnp.int32, (rows_all, lanes), 0)
+        == jnp.broadcast_to(picks_ref[...], (rows_all, lanes))
     ).astype(F32)
-    acc_ref[...] += jnp.dot(part, hot, precision=HIGHEST, preferred_element_type=F32)
-
-    @pl.when(step == pl.num_programs(0) - 1)
-    def _():
-        halves = lanes // 128
-        for i in range(modes // 8):
-            for h in range(halves):
-                out_ref[i * halves + h] = acc_ref[pl.ds(8 * i, 8), pl.ds(128 * h, 128)]
-
-
-def project(snapshots, basis, kappa, low, high, picks_row):
-    count, nv, nx, ny, nz = snapshots.shape
-    modes = basis.shape[0]
-    lanes = picks_row.shape[1]
-    chunks = (modes // 8) * (lanes // 128)
-    whole = lambda a: pl.BlockSpec(a.shape, lambda i: (0,) * a.ndim)
-    return pl.pallas_call(
-        functools.partial(project_kernel, count),
-        grid=(-(-count // CHUNK),),
-        out_shape=jax.ShapeDtypeStruct((chunks, 8, 128), F32),
-        in_specs=[
-            pl.BlockSpec((CHUNK, nv, nx, ny, nz), lambda i: (i, 0, 0, 0, 0)),
-            whole(basis), whole(kappa), whole(low), whole(high), whole(picks_row),
-        ],
-        out_specs=pl.BlockSpec((chunks, 8, 128), lambda i: (0, 0, 0)),
-        scratch_shapes=[
-            pltpu.VMEM((2 * modes * ny, nv * nx * nz), BF16),
-            pltpu.VMEM((modes, lanes), F32),
-        ],
-        compiler_params=pltpu.CompilerParams(vmem_limit_bytes=48 * 2**20),
-        name="project",
-    )(snapshots, basis, kappa, low, high, picks_row)
-
-
-def share_kernel(n_tm, n_space, own_ref, all_ref, land_ref, send1, recv1, send2, recv2):
-    chunks = own_ref.shape[0]
-    tm = lax.axis_index("tm")
-    sp = lax.axis_index("space")
-    me = tm * n_space + sp
-    total = n_tm * n_space
-
-    def peer(i):
-        other = lax.rem(me + i, total)
-        return other // n_space, lax.rem(other, n_space)
-
-    barrier = pltpu.get_barrier_semaphore()
-
-    def greet(i, carry):
-        pl.semaphore_signal(barrier, inc=1, device_id=peer(i), device_id_type=MESH)
-        return carry
-
-    lax.fori_loop(1, total, greet, 0)
-    pl.semaphore_wait(barrier, total - 1)
+    mine = jnp.dot(part, hot, precision=HIGHEST, preferred_element_type=F32)
+    halves = lanes // 128
+    for i in range(modes // 8):
+        for h in range(halves):
+            own_ref[i * halves + h] = mine[8 * i : 8 * i + 8, 128 * h : 128 * h + 128]
 
     def part_to(owner):
-        return pltpu.make_async_remote_copy(
-            src_ref=own_ref.at[owner], dst_ref=land_ref.at[sp],
-            send_sem=send1.at[owner], recv_sem=recv1.at[sp],
-            device_id=(tm, owner), device_id_type=MESH,
-        )
-
-    def part_from(source):
-        return pltpu.make_async_remote_copy(
-            src_ref=own_ref.at[0], dst_ref=land_ref.at[source],
-            send_sem=send1.at[0], recv_sem=recv1.at[source],
-            device_id=(tm, source), device_id_type=MESH,
-        )
+        return remote(own_ref.at[owner], land_ref.at[sp], send1.at[owner], recv1.at[sp], (tm, owner))
 
     for owner in range(chunks):
         @pl.when(sp != owner)
         def _():
             part_to(owner).start()
+
+    def give_to(i):
+        return remote(
+            all_ref.at[tm, sp], all_ref.at[tm, sp], send2.at[i], recv2.at[tm * chunks + sp], peer(i)
+        )
 
     @pl.when(sp < chunks)
     def _():
@@ -151,21 +195,29 @@
         for source in range(n_space):
             @pl.when(sp != source)
             def _():
-                part_from(source).wait_recv()
+                remote(
+                    own_ref.at[0], land_ref.at[source], send1.at[0], recv1.at[source], (tm, source)
+                ).wait_recv()
         total_sum = land_ref[0]
         for source in range(1, n_space):
             total_sum = total_sum + land_ref[source]
         all_ref[tm, sp] = total_sum
 
         def give(i, carry):
-            pltpu.make_async_remote_copy(
-                src_ref=all_ref.at[tm, sp], dst_ref=all_ref.at[tm, sp],
-                send_sem=send2.at[i], recv_sem=recv2.at[tm * chunks + sp],
-                device_id=peer(i), device_id_type=MESH,
-            ).start()
+            give_to(i).start()
             return carry
 
         lax.fori_loop(1, total, give, 0)
+
+    for side in range(2):
+        @pl.when(sends[side])
+        def _():
+            for copy in plane_copies(side):
+                copy.wait_send()
+
+        @pl.when(receives[side])
+        def _():
+            forward(side).wait_send()
 
     for owner in range(chunks):
         @pl.when(sp != owner)
@@ -176,43 +228,49 @@
         for owner in range(chunks):
             @pl.when(jnp.logical_or(tm != group, sp != owner))
             def _():
-                pltpu.make_async_remote_copy(
-                    src_ref=all_ref.at[group, owner], dst_ref=all_ref.at[group, owner],
-                    send_sem=send2.at[0], recv_sem=recv2.at[group * chunks + owner],
-                    device_id=(group, owner), device_id_type=MESH,
+                remote(
+                    all_ref.at[group, owner], all_ref.at[group, owner],
+                    send2.at[0], recv2.at[group * chunks + owner], (group, owner),
                 ).wait_recv()
 
     @pl.when(sp < chunks)
     def _():
         def done(i, carry):
-            pltpu.make_async_remote_copy(
-                src_ref=all_ref.at[tm, sp], dst_ref=all_ref.at[tm, sp],
-                send_sem=send2.at[i], recv_sem=recv2.at[tm * chunks + sp],
-                device_id=peer(i), device_id_type=MESH,
-            ).wait_send()
+            give_to(i).wait_send()
             return carry
 
         lax.fori_loop(1, total, done, 0)
 
 
-def share(own, n_tm, n_space):
-    chunks = own.shape[0]
-    total = n_tm * n_space
+def gather_coefficients(snapshots, basis, kappa, picks_row, n_tm, n_space):
+    count, nv, nx, ny, nz = snapshots.shape
+    modes = basis.shape[0]
+    lanes = picks_row.shape[1]
+    chunks = (modes // 8) * (lanes // 128)
+    rows_all = -(-count // CHUNK) * CHUNK
+    vmem = pl.BlockSpec(memory_space=pltpu.VMEM)
+    dma = pltpu.SemaphoreType.DMA
     return pl.pallas_call(
-        functools.partial(share_kernel, n_tm, n_space),
+        functools.partial(gather_kernel, n_tm, n_space, chunks),
         out_shape=jax.ShapeDtypeStruct((n_tm, chunks, 8, 128), F32),
-        in_specs=[pl.BlockSpec(memory_space=pltpu.VMEM)],
-        out_specs=pl.BlockSpec(memory_space=pltpu.VMEM),
+        in_specs=[pl.BlockSpec(memory_space=pl.ANY), vmem, vmem, vmem],
+        out_specs=vmem,
         scratch_shapes=[
+            pltpu.VMEM((rows_all, nv, nx, ny, nz), BF16),
+            pltpu.VMEM((2 * modes * ny, nv * nx * nz), BF16),
+            pltpu.VMEM((rows_all, modes * ny), F32),
+            pltpu.VMEM((2, modes, nv, ny, nz), BF16),
+            pltpu.VMEM((2, nv, ny, nz), F32),
+            pltpu.VMEM((chunks, 8, 128), F32),
             pltpu.VMEM((n_space, 8, 128), F32),
-            pltpu.SemaphoreType.DMA((chunks,)),
-            pltpu.SemaphoreType.DMA((n_space,)),
-            pltpu.SemaphoreType.DMA((total,)),
-            pltpu.SemaphoreType.DMA((n_tm * chunks,)),
+            dma, dma((2,)), dma((2,)), dma((2,)), dma((2,)), dma((2,)), dma((2,)),
+            dma((chunks,)), dma((n_space,)), dma((n_tm * n_space,)), dma((n_tm * chunks,)),
         ],
-        compiler_params=pltpu.CompilerParams(collective_id=0, has_side_effects=True),
-        name="share",
-    )(own)
+        compiler_params=pltpu.CompilerParams(
+            collective_id=0, has_side_effects=True, vmem_limit_bytes=48 * 2**20
+        ),
+        name="gather_coefficients",
+    )(snapshots, basis, kappa, picks_row)
 
 
 def eliminate(a, b):
@@ -395,22 +453,9 @@
 def body(snapshots, picks, basis, kappa):
     n_tm, n_space = lax.axis_size("tm"), lax.axis_size("space")
     modes, count = basis.shape[0], picks.shape[0]
-    hi = lax.reduce_precision(kappa, 8, 7)
-    mid = lax.reduce_precision(kappa - hi, 8, 7)
-    low = kappa - hi - mid
-    parts = jnp.stack([hi, mid, low]).astype(BF16)
-
-    def plane(x):
-        return jnp.concatenate([basis[:, :, x], parts[:, :, x]], axis=0)
-
-    forward = [(i, i + 1) for i in range(n_space - 1)]
-    backward = [(i + 1, i) for i in range(n_space - 1)]
-    from_low = lax.ppermute(plane(basis.shape[2] - 1), "space", forward)
-    from_high = lax.ppermute(plane(0), "space", backward)
     lanes = -(-count // 128) * 128
     picks_row = jnp.pad(picks, (0, lanes - count), constant_values=-1).reshape(1, lanes)
-    own = project(snapshots, basis, kappa, from_low, from_high, picks_row)
-    shared = share(own, n_tm, n_space)
+    shared = gather_coefficients(snapshots, basis, kappa, picks_row, n_tm, n_space)
     return tuple(factorize(shared, count, modes))
 
 

time: 82 us -> 68.7 us (0.84)
  waiting for transfers between devices: 13.2 us -> 0 us
  Pallas kernels: 54.6 us -> 62.1 us
  starting transfers between devices: 6.19 us -> 0 us
  other arithmetic: 0.92 us -> 0 us
    ppermute x2 -> x0, waiting for transfers between devices: 13.2 us -> none  [the longest x1 13.2 us: body(): from_low = lax.ppermute(plane(basis.shape[2] - 1), 'space', forward)]
    pallas_call x2 -> x1, Pallas kernels: 25.7 us -> 33.1 us  [gather_coefficients(): pl.pallas_call(functools.partial(gather_kernel, n_tm, n_space, chunks), o...]
    ppermute x2 -> x0, starting transfers between devices: 6.19 us -> none  [the longest x1 4.89 us: body(): from_low = lax.ppermute(plane(basis.shape[2] - 1), 'space', forward)]
    squeeze x2 -> x0, local copies, waits for them, and re-layouts: 1.14 us -> none  [plane(): return jnp.concatenate([basis[:, :, x], parts[:, :, x]], axis=0)]
    unnamed x12 -> x10, local copies, waits for them, and re-layouts: 3.39 us -> 4.33 us
    another operation x2 -> x0, other arithmetic: 0.85 us -> none  [body(): parts = jnp.stack([hi, mid, low]).astype(BF16)]
  transfers between devices with their start and end apart: 2 -> 0, of which waited for: 1 -> 0; matrix products, arithmetic and copies ran while one was open for 1% -> 0% of each run, Pallas kernels for 0% -> 0%
where the time goes in v1:
time: 68.7 us; the launch traced here: 68.4 us
  Pallas kernels  62.1 us (90%)
  local copies, waits for them, and re-layouts  5.71 us (8%)
    pallas_call x1, Pallas kernels, gather_coefficients(): pl.pallas_call(functools.partial(gather_kernel, n_tm, n_space, chunks), o...  33.1 us
    pallas_call x1, Pallas kernels, factorize(): pl.pallas_call(functools.partial(factor_kernel, count, n_feat), out_shape...  29 us
    unnamed x10, local copies, waits for them, and re-layouts  4.33 us

profile of v1, /device:TPU:0, one launch (start us, length us, event | category | flops | bytes accessed | tf_op | source)
XLA Modules:
  0.0 68.4 jit_solution(12248558058851576733)
XLA Ops:
  0.6 0.7 pad.4
  1.3 0.0 copy-start
  1.3 2.5 %copy-done = bf16[252,5,2,8,128]{4,3,2,1,0:T(8,128)(2,1)S(1)} copy-done((bf16[252,5,2,8,128]{4,3,2,1,0:T(8,128)(2,1)S(1)}, bf16[252,5,2,8,128]{4,3,2,1,0:T(8,128)(2,1)}, u32[]{:S(2)}) %copy-start) | copy-done | bytes 5160984
  3.8 0.0 copy-start.1
  3.8 1.1 %copy-done.1 = bf16[32,5,2,8,128]{4,3,2,1,0:T(8,128)(2,1)S(1)} copy-done((bf16[32,5,2,8,128]{4,3,2,1,0:T(8,128)(2,1)S(1)}, bf16[32,5,2,8,128]{4,3,2,1,0:T(8,128)(2,1)}, u32[]{:S(2)}) %copy-start.1) | copy-done | bytes 655384
  4.9 0.0 copy-start.4
  4.9 0.8 %copy-done.4 = f32[5,2,8,128]{3,2,1,0:T(8,128)S(1)} copy-done((f32[5,2,8,128]{3,2,1,0:T(8,128)S(1)}, f32[5,2,8,128]{3,2,1,0:T(8,128)}, u32[]{:S(2)}) %copy-start.4) | copy-done | bytes 40984
  5.6 0.0 copy-start.2
  5.6 0.0 copy-start.3
  5.6 33.1 %gather_coefficients.1.all_ref = f32[4,8,8,128]{3,2,1,0:T(8,128)S(1)} custom-call(bf16[252,5,2,8,128]{4,3,2,1,0:T(8,128)(2,1)S(1)} %copy-done, bf16[32,5,2,8,128]{4,3,2,1,0:T(8,128)(2,1)S(1)} %copy-done.1, f32[5,2,8,128]{3,2,1,0:T(8,128)S(1)} %copy-done.4, s32[1,256]{1,0:T(1,128)S(1)} %bitcast.1), custom_call_target="tpu_custom_call" | custom-call | tf_op jit(solution)/shard_map/gather_coefficients/pallas_call | solution.py:253
  38.7 0.0 copy-done.2
  38.7 0.0 copy-done.3
  38.7 29.0 %factorize.1 = (f32[224,32]{1,0:T(8,128)S(1)}, f32[561,561]{1,0:T(8,128)}) custom-call(f32[4,8,8,128]{3,2,1,0:T(8,128)S(1)} %gather_coefficients.1.all_ref, bf16[640,128]{1,0:T(8,128)(2,1)S(1)} %copy-done.3, bf16[640,128]{1,0:T(8,128)(2,1)S(1)} %copy-done.2), custom_call_target="tpu_custom_call" | custom-call | tf_op jit(solution)/shard_map/factorize/pallas_call | solution.py:434
  67.7 0.7 %copy.8 = f32[224,32]{0,1:T(8,128)} copy(f32[224,32]{1,0:T(8,128)S(1)} %get-tuple-element.2) | data formatting | bytes 57344 | tf_op jit(solution)/shard_map/factorize/pallas_call | solution.py:434
Async XLA Ops:
  1.3 2.5 %copy-start = (bf16[252,5,2,8,128]{4,3,2,1,0:T(8,128)(2,1)S(1)}, bf16[252,5,2,8,128]{4,3,2,1,0:T(8,128)(2,1)}, u32[]{:S(2)}) copy-start(bf16[252,5,2,8,128]{4,3,2,1,0:T(8,128)(2,1)} %s_any.1) | copy-start | bytes 15482884
  3.8 1.1 %copy-start.1 = (bf16[32,5,2,8,128]{4,3,2,1,0:T(8,128)(2,1)S(1)}, bf16[32,5,2,8,128]{4,3,2,1,0:T(8,128)(2,1)}, u32[]{:S(2)}) copy-start(bf16[32,5,2,8,128]{4,3,2,1,0:T(8,128)(2,1)} %b_ref.1) | copy-start | bytes 1966084
  4.9 0.8 %copy-start.4 = (f32[5,2,8,128]{3,2,1,0:T(8,128)S(1)}, f32[5,2,8,128]{3,2,1,0:T(8,128)}, u32[]{:S(2)}) copy-start(f32[5,2,8,128]{3,2,1,0:T(8,128)} %k_ref.1) | copy-start | bytes 122884
  5.6 33.1 %copy-start.2 = (bf16[640,128]{1,0:T(8,128)(2,1)S(1)}, bf16[640,128]{1,0:T(8,128)(2,1)}, u32[]{:S(2)}) copy-start(bf16[640,128]{1,0:T(8,128)(2,1)} %constant.7.clone.s2_ref) | copy-start | bytes 491524
  5.6 33.1 %copy-start.3 = (bf16[640,128]{1,0:T(8,128)(2,1)S(1)}, bf16[640,128]{1,0:T(8,128)(2,1)}, u32[]{:S(2)}) copy-start(bf16[640,128]{1,0:T(8,128)(2,1)} %constant.6.clone.s1_ref) | copy-start | bytes 491524

commit v2 on v1

--- a/solution.py
+++ b/solution.py
@@ -12,20 +12,20 @@
 HIGHEST = lax.Precision.HIGHEST
 NT = (((1,), (1,)), ((), ()))
 TN = (((0,), (0,)), ((), ()))
-CHUNK = 64
+CHUNK = 128
 F32 = jnp.float32
 BF16 = jnp.bfloat16
 
 
 def gather_kernel(
-    n_tm, n_space, chunks, s_any, b_ref, k_ref, picks_ref, all_ref,
-    s_ref, g_ref, z_ref, hb_ref, hk_ref, own_ref, land_ref,
-    load, send_b, recv_b, send_k, recv_k, send_f, recv_f, send1, recv1, send2, recv2,
+    n_tm, n_space, chunks, s_any, b_any, k_any, picks_ref, all_ref,
+    s_ref, b_ref, k_ref, g_ref, z_ref, hb_ref, hk_ref, own_ref, land_ref,
+    load, load_b, load_k, send_b, recv_b, send_k, recv_k, send_f, recv_f, send1, recv1, send2, recv2,
 ):
     count, nv, nx, ny, nz = s_any.shape
-    modes = b_ref.shape[0]
+    modes = b_any.shape[0]
     wide, half = modes * ny, modes // 2
-    lanes = picks_ref.shape[1]
+    taken = picks_ref.shape[1]
     rows_all = s_ref.shape[0]
     tm = lax.axis_index("tm")
     sp = lax.axis_index("space")
@@ -38,6 +38,10 @@
         other = lax.rem(me + i, total)
         return other // n_space, lax.rem(other, n_space)
 
+    loading_b = pltpu.make_async_copy(b_any, b_ref, load_b)
+    loading_k = pltpu.make_async_copy(k_any, k_ref, load_k)
+    loading_b.start()
+    loading_k.start()
     loading = pltpu.make_async_copy(s_any, s_ref.at[pl.ds(0, count)], load)
     loading.start()
     barrier = pltpu.get_barrier_semaphore()
@@ -60,8 +64,8 @@
         to = lax.rem(sp + (1 if side == 0 else n_space - 1), n_space)
         mine = pl.ds(core * half, half)
         return (
-            remote(b_ref.at[mine, :, x], hb_ref.at[side, mine], send_b.at[side], recv_b.at[side], (tm, to)),
-            remote(k_ref.at[:, x], hk_ref.at[side], send_k.at[side], recv_k.at[side], (tm, to)),
+            remote(b_any.at[mine, :, x], hb_ref.at[side, mine], send_b.at[side], recv_b.at[side], (tm, to)),
+            remote(k_any.at[:, x], hk_ref.at[side], send_k.at[side], recv_k.at[side], (tm, to)),
         )
 
     def forward(side):
@@ -94,6 +98,8 @@
     def spread(plane, many):
         return jnp.broadcast_to(plane[None], (many, ny, nz)).reshape(many * ny, nz)
 
+    loading_b.wait()
+    loading_k.wait()
     yi = lax.broadcasted_iota(jnp.int32, (wide, nz), 0) % ny
     zi = lax.broadcasted_iota(jnp.int32, (wide, nz), 1)
     for v in range(nv):
@@ -167,14 +173,17 @@
     ).astype(F32)
     part = lax.dot_general(fold, z_ref[...], NT, precision=HIGHEST, preferred_element_type=F32)
     hot = (
-        lax.broadcasted_iota(jnp.int32, (rows_all, lanes), 0)
-        == jnp.broadcast_to(picks_ref[...], (rows_all, lanes))
+        lax.broadcasted_iota(jnp.int32, (rows_all, taken), 0)
+        == jnp.broadcast_to(picks_ref[...], (rows_all, taken))
     ).astype(F32)
     mine = jnp.dot(part, hot, precision=HIGHEST, preferred_element_type=F32)
-    halves = lanes // 128
+    halves = -(-taken // 128)
     for i in range(modes // 8):
         for h in range(halves):
-            own_ref[i * halves + h] = mine[8 * i : 8 * i + 8, 128 * h : 128 * h + 128]
+            width = min(128, taken - 128 * h)
+            if width < 128:
+                own_ref[i * halves + h] = jnp.zeros((8, 128), F32)
+            own_ref[i * halves + h, :, pl.ds(0, width)] = mine[8 * i : 8 * i + 8, 128 * h : 128 * h + width]
 
     def part_to(owner):
         return remote(own_ref.at[owner], land_ref.at[sp], send1.at[owner], recv1.at[sp], (tm, owner))
@@ -245,25 +254,26 @@
 def gather_coefficients(snapshots, basis, kappa, picks_row, n_tm, n_space):
     count, nv, nx, ny, nz = snapshots.shape
     modes = basis.shape[0]
-    lanes = picks_row.shape[1]
-    chunks = (modes // 8) * (lanes // 128)
+    chunks = (modes // 8) * -(-picks_row.shape[1] // 128)
     rows_all = -(-count // CHUNK) * CHUNK
     vmem = pl.BlockSpec(memory_space=pltpu.VMEM)
     dma = pltpu.SemaphoreType.DMA
     return pl.pallas_call(
         functools.partial(gather_kernel, n_tm, n_space, chunks),
         out_shape=jax.ShapeDtypeStruct((n_tm, chunks, 8, 128), F32),
-        in_specs=[pl.BlockSpec(memory_space=pl.ANY), vmem, vmem, vmem],
+        in_specs=[pl.BlockSpec(memory_space=pltpu.HBM)] * 3 + [vmem],
         out_specs=vmem,
         scratch_shapes=[
             pltpu.VMEM((rows_all, nv, nx, ny, nz), BF16),
+            pltpu.VMEM(basis.shape, BF16),
+            pltpu.VMEM(kappa.shape, F32),
             pltpu.VMEM((2 * modes * ny, nv * nx * nz), BF16),
             pltpu.VMEM((rows_all, modes * ny), F32),
             pltpu.VMEM((2, modes, nv, ny, nz), BF16),
             pltpu.VMEM((2, nv, ny, nz), F32),
             pltpu.VMEM((chunks, 8, 128), F32),
             pltpu.VMEM((n_space, 8, 128), F32),
-            dma, dma((2,)), dma((2,)), dma((2,)), dma((2,)), dma((2,)), dma((2,)),
+            dma, dma, dma, dma((2,)), dma((2,)), dma((2,)), dma((2,)), dma((2,)), dma((2,)),
             dma((chunks,)), dma((n_space,)), dma((n_tm * n_space,)), dma((n_tm * chunks,)),
         ],
         compiler_params=pltpu.CompilerParams(
@@ -271,6 +281,12 @@
         ),
         name="gather_coefficients",
     )(snapshots, basis, kappa, picks_row)
+
+
+def reciprocal(x):
+    r = pl.reciprocal(x, approx=True)
+    r = r * (2.0 - x * r)
+    return r * (2.0 - x * r)
 
 
 def eliminate(a, b):
@@ -283,15 +299,17 @@
         cols = [column_of(a[s], 8 * s + k) for k in range(8)]
         inv, known, a_rows, b_rows = [], [], [], []
         d = jnp.ones((8, 128), F32)
+        e = jnp.ones((8, 128), F32)
         for k in range(8):
             pivot = row_of(cols[k], k)
-            d = jnp.where(sub == k, pivot, d)
-            r = 1.0 / pivot
-            m = jnp.where(sub > k, cols[k] * r, 0.0)
+            r = reciprocal(pivot)
             seen = {}
             for q in range(k + 1, 8):
                 seen[q] = row_of(cols[q], k)
-                cols[q] = cols[q] - m * seen[q]
+                cols[q] = cols[q] - (cols[k] * seen[q]) * r
+            d = jnp.where(sub == k, pivot, d)
+            e = jnp.where(sub == k, r, e)
+            m = jnp.where(sub > k, cols[k] * r, 0.0)
             a_rows.append(row_of(a[s], k))
             a[s] = a[s] - m * a_rows[k]
             if b is not None:
@@ -300,12 +318,18 @@
             inv.append(r)
             known.append(seen)
         diag.append(d)
+        if s + 2 < tiles:
+            turned = jnp.transpose(a[s] * e)
         for i in range(s + 1, tiles):
-            cols = [column_of(a[i], 8 * s + k) for k in range(8)]
+            if i == s + 1:
+                cols = [column_of(a[i], 8 * s + k) for k in range(8)]
             for k in range(8):
-                m = cols[k] * inv[k]
-                for q in range(k + 1, 8):
-                    cols[q] = cols[q] - m * known[k][q]
+                if i == s + 1:
+                    m = cols[k] * inv[k]
+                    for q in range(k + 1, 8):
+                        cols[q] = cols[q] - m * known[k][q]
+                else:
+                    m = column_of(turned[8 * i : 8 * i + 8, :], k)
                 a[i] = a[i] - m * a_rows[k]
                 if b is not None:
                     b[i] = b[i] - m * b_rows[k]
@@ -316,7 +340,12 @@
     return a, b, scale
 
 
-def factor_kernel(count, n_feat, all_ref, s1_ref, s2_ref, c_ref, o_ref, f_ref, a_ref, u_ref, l_ref):
+def split(x):
+    hi = x.astype(BF16)
+    return hi, (x - hi.astype(F32)).astype(BF16)
+
+
+def factor_kernel(count, n_feat, all_ref, s1_ref, s2_ref, c_ref, o_ref, fa_ref, fb_ref, a_ref, u_ref, l_ref):
     n_tm, chunks = all_ref.shape[:2]
     padded = s1_ref.shape[0]
     blocks = padded // 128
@@ -335,7 +364,7 @@
             axis=0,
         )
 
-    c_ref[...] = jnp.transpose(coeffs(tm))[:count, :]
+    c_ref[...] = coeffs(tm)[:, :count]
     lane = lax.broadcasted_iota(jnp.int32, (modes, lanes), 1)
     top = lax.broadcasted_iota(jnp.int32, (modes, lanes), 0)
     ones = jnp.where(jnp.logical_and(lane < count, top == 0), 1.0, 0.0).astype(BF16)
@@ -348,13 +377,20 @@
         stack = jnp.concatenate([hi, mid, low, ones], axis=0)
         f1 = jnp.dot(s1_ref[...], stack, preferred_element_type=F32)
         f2 = jnp.dot(s2_ref[...], stack, preferred_element_type=F32)
-        f_ref[:, pl.ds(g * lanes, lanes)] = f1 * f2
+        fh, fl = split(f1 * f2)
+        at = [pl.ds((part * n_tm + g) * lanes, lanes) for part in range(3)]
+        fa_ref[:, at[0]] = fh
+        fa_ref[:, at[1]] = fh
+        fa_ref[:, at[2]] = fl
+        fb_ref[:, at[0]] = fh
+        fb_ref[:, at[1]] = fl
+        fb_ref[:, at[2]] = fh
 
     share_of = 1.0 / (count * n_tm)
     for j in range(blocks):
         gram = lax.dot_general(
-            f_ref[pl.ds(j * 128, 128), :], f_ref[pl.ds(j * 128, padded - j * 128), :], NT,
-            precision=HIGHEST, preferred_element_type=F32,
+            fa_ref[pl.ds(j * 128, 128), :], fb_ref[pl.ds(j * 128, padded - j * 128), :], NT,
+            preferred_element_type=F32,
         )
         a_ref[pl.ds(j * 128, 128), pl.ds(j * 128, padded - j * 128)] = gram * share_of
 
@@ -385,16 +421,20 @@
                 if jj > 0:
                     o_ref[pl.ds(here, 128), pl.ds(0, here)] = jnp.zeros((128, here), F32)
                 o_ref[pl.ds(here, 128), pl.ds(here, 128)] = u_ref[...]
+                lh, ll = split(l_ref[...])
+                ah, al = split(a_ref[pl.ds(here, 128), pl.ds(after, padded - after)])
                 w = jnp.dot(
-                    l_ref[...], a_ref[pl.ds(here, 128), pl.ds(after, padded - after)],
-                    precision=HIGHEST, preferred_element_type=F32,
+                    jnp.concatenate([lh, lh, ll], axis=1), jnp.concatenate([ah, al, ah], axis=0),
+                    preferred_element_type=F32,
                 )
+                wh, wl = split(w)
+                left, right = jnp.concatenate([wh, wh, wl], axis=0), jnp.concatenate([wh, wl, wh], axis=0)
                 o_ref[pl.ds(here, 128), pl.ds(after, n_feat - after)] = w[:, : n_feat - after]
                 for i in range(jj + 1, blocks):
                     row = i * 128
                     a_ref[pl.ds(row, 128), pl.ds(row, padded - row)] -= lax.dot_general(
-                        w[:, row - after : row - after + 128], w[:, row - after :], TN,
-                        precision=HIGHEST, preferred_element_type=F32,
+                        left[:, row - after : row - after + 128], right[:, row - after :], TN,
+                        preferred_element_type=F32,
                     )
         return carry
 
@@ -434,13 +474,14 @@
     return pl.pallas_call(
         functools.partial(factor_kernel, count, n_feat),
         out_shape=(
-            jax.ShapeDtypeStruct((count, modes), F32),
+            jax.ShapeDtypeStruct((modes, count), F32),
             jax.ShapeDtypeStruct((n_feat, n_feat), F32),
         ),
         in_specs=[vmem] * 3,
         out_specs=(vmem, vmem),
         scratch_shapes=[
-            pltpu.VMEM((padded, n_tm * lanes), F32),
+            pltpu.VMEM((padded, 3 * n_tm * lanes), BF16),
+            pltpu.VMEM((padded, 3 * n_tm * lanes), BF16),
             pltpu.VMEM((padded, padded), F32),
             pltpu.VMEM((128, 128), F32),
             pltpu.VMEM((128, 128), F32),
@@ -453,10 +494,9 @@
 def body(snapshots, picks, basis, kappa):
     n_tm, n_space = lax.axis_size("tm"), lax.axis_size("space")
     modes, count = basis.shape[0], picks.shape[0]
-    lanes = -(-count // 128) * 128
-    picks_row = jnp.pad(picks, (0, lanes - count), constant_values=-1).reshape(1, lanes)
-    shared = gather_coefficients(snapshots, basis, kappa, picks_row, n_tm, n_space)
-    return tuple(factorize(shared, count, modes))
+    shared = gather_coefficients(snapshots, basis, kappa, picks.reshape(1, count), n_tm, n_space)
+    coefficients, factor = factorize(shared, count, modes)
+    return coefficients.T, factor
 
 
 def solution(mesh):

time: 68.7 us -> 68.6 us (level)
  local copies, waits for them, and re-layouts: 5.71 us -> 5.01 us
    pallas_call x1, Pallas kernels: 29 us -> 29.7 us  [factorize(): pl.pallas_call(functools.partial(factor_kernel, count, n_feat), out_shape...]
    pallas_call x1 -> x0, local copies, waits for them, and re-layouts: 0.69 us -> none  [factorize(): pl.pallas_call(functools.partial(factor_kernel, count, n_feat), out_shape...]
    unnamed x10 -> x12, local copies, waits for them, and re-layouts: 4.33 us -> 5.01 us
where the time goes in v2:
time: 68.6 us; the launch traced here: 68.3 us
  Pallas kernels  62.6 us (91%)
  local copies, waits for them, and re-layouts  5.01 us (7%)
    pallas_call x1, Pallas kernels, gather_coefficients(): pl.pallas_call(functools.partial(gather_kernel, n_tm, n_space, chunks), o...  32.9 us
    pallas_call x1, Pallas kernels, factorize(): pl.pallas_call(functools.partial(factor_kernel, count, n_feat), out_shape...  29.7 us
    unnamed x12, local copies, waits for them, and re-layouts  5.01 us

profile of v2, /device:TPU:0, one launch (start us, length us, event | category | flops | bytes accessed | tf_op | source)
XLA Modules:
  0.0 68.3 jit_solution(9807458049086792483)
XLA Ops:
  0.6 0.0 copy-start
  0.6 2.5 %copy-done = bf16[252,5,2,8,128]{4,3,2,1,0:T(8,128)(2,1)S(1)} copy-done((bf16[252,5,2,8,128]{4,3,2,1,0:T(8,128)(2,1)S(1)}, bf16[252,5,2,8,128]{4,3,2,1,0:T(8,128)(2,1)}, u32[]{:S(2)}) %copy-start) | copy-done | bytes 5160984
  3.1 0.0 copy-start.1
  3.1 1.1 %copy-done.1 = bf16[32,5,2,8,128]{4,3,2,1,0:T(8,128)(2,1)S(1)} copy-done((bf16[32,5,2,8,128]{4,3,2,1,0:T(8,128)(2,1)S(1)}, bf16[32,5,2,8,128]{4,3,2,1,0:T(8,128)(2,1)}, u32[]{:S(2)}) %copy-start.1) | copy-done | bytes 655384
  4.2 0.0 copy-start.4
  4.2 0.8 %copy-done.4 = f32[5,2,8,128]{3,2,1,0:T(8,128)S(1)} copy-done((f32[5,2,8,128]{3,2,1,0:T(8,128)S(1)}, f32[5,2,8,128]{3,2,1,0:T(8,128)}, u32[]{:S(2)}) %copy-start.4) | copy-done | bytes 40984
  5.0 0.0 copy-start.5
  5.0 0.7 copy-done.5
  5.6 0.0 copy-start.2
  5.6 0.0 copy-start.3
  5.6 32.9 %gather_coefficients.1.all_ref = f32[4,8,8,128]{3,2,1,0:T(8,128)S(1)} custom-call(bf16[252,5,2,8,128]{4,3,2,1,0:T(8,128)(2,1)S(1)} %copy-done, bf16[32,5,2,8,128]{4,3,2,1,0:T(8,128)(2,1)S(1)} %copy-done.1, f32[5,2,8,128]{3,2,1,0:T(8,128)S(1)} %copy-done.4, s32[1,224]{1,0:T(1,128)S(1)} %bitcast.2), custom_call_target="tpu_custom_call" | custom-call | tf_op jit(solution)/shard_map/gather_coefficients/pallas_call | solution.py:261
  38.6 0.0 copy-done.2
  38.6 0.0 copy-done.3
  38.6 29.7 %factorize.1 = (f32[32,224]{1,0:T(8,128)}, f32[561,561]{1,0:T(8,128)}) custom-call(f32[4,8,8,128]{3,2,1,0:T(8,128)S(1)} %gather_coefficients.1.all_ref, bf16[640,128]{1,0:T(8,128)(2,1)S(1)} %copy-done.3, bf16[640,128]{1,0:T(8,128)(2,1)S(1)} %copy-done.2), custom_call_target="tpu_custom_call" | custom-call | tf_op jit(solution)/shard_map/factorize/pallas_call | solution.py:474
Async XLA Ops:
  0.6 2.5 %copy-start = (bf16[252,5,2,8,128]{4,3,2,1,0:T(8,128)(2,1)S(1)}, bf16[252,5,2,8,128]{4,3,2,1,0:T(8,128)(2,1)}, u32[]{:S(2)}) copy-start(bf16[252,5,2,8,128]{4,3,2,1,0:T(8,128)(2,1)} %s_any.1) | copy-start | bytes 15482884
  3.1 1.1 %copy-start.1 = (bf16[32,5,2,8,128]{4,3,2,1,0:T(8,128)(2,1)S(1)}, bf16[32,5,2,8,128]{4,3,2,1,0:T(8,128)(2,1)}, u32[]{:S(2)}) copy-start(bf16[32,5,2,8,128]{4,3,2,1,0:T(8,128)(2,1)} %b_any.1) | copy-start | bytes 1966084
  4.2 0.8 %copy-start.4 = (f32[5,2,8,128]{3,2,1,0:T(8,128)S(1)}, f32[5,2,8,128]{3,2,1,0:T(8,128)}, u32[]{:S(2)}) copy-start(f32[5,2,8,128]{3,2,1,0:T(8,128)} %k_any.1) | copy-start | bytes 122884
  5.0 0.7 copy-start.5
  5.6 32.9 %copy-start.2 = (bf16[640,128]{1,0:T(8,128)(2,1)S(1)}, bf16[640,128]{1,0:T(8,128)(2,1)}, u32[]{:S(2)}) copy-start(bf16[640,128]{1,0:T(8,128)(2,1)} %constant.5.clone.s2_ref) | copy-start | bytes 491524
  5.6 32.9 %copy-start.3 = (bf16[640,128]{1,0:T(8,128)(2,1)S(1)}, bf16[640,128]{1,0:T(8,128)(2,1)}, u32[]{:S(2)}) copy-start(bf16[640,128]{1,0:T(8,128)(2,1)} %constant.4.clone.s1_ref) | copy-start | bytes 491524

commit v3 on v2

--- a/solution.py
+++ b/solution.py
@@ -277,7 +277,7 @@
             dma((chunks,)), dma((n_space,)), dma((n_tm * n_space,)), dma((n_tm * chunks,)),
         ],
         compiler_params=pltpu.CompilerParams(
-            collective_id=0, has_side_effects=True, vmem_limit_bytes=48 * 2**20
+            collective_id=0, has_side_effects=True, vmem_limit_bytes=60 * 2**20
         ),
         name="gather_coefficients",
     )(snapshots, basis, kappa, picks_row)
@@ -285,54 +285,72 @@
 
 def reciprocal(x):
     r = pl.reciprocal(x, approx=True)
-    r = r * (2.0 - x * r)
     return r * (2.0 - x * r)
+
+
+def parts_of(x):
+    hi = x.astype(BF16).astype(F32)
+    return hi, x - hi
 
 
 def eliminate(a, b):
     tiles = len(a)
     sub = lax.broadcasted_iota(jnp.int32, (8, 128), 0)
+    zero = jnp.zeros((8, 128), F32)
     row_of = lambda x, k: jnp.broadcast_to(x[k : k + 1, :], (8, 128))
     column_of = lambda x, k: jnp.broadcast_to(x[:, k : k + 1], (8, 128))
     diag = []
     for s in range(tiles):
         cols = [column_of(a[s], 8 * s + k) for k in range(8)]
-        inv, known, a_rows, b_rows = [], [], [], []
-        d = jnp.ones((8, 128), F32)
-        e = jnp.ones((8, 128), F32)
-        for k in range(8):
-            pivot = row_of(cols[k], k)
-            r = reciprocal(pivot)
-            seen = {}
-            for q in range(k + 1, 8):
-                seen[q] = row_of(cols[q], k)
-                cols[q] = cols[q] - (cols[k] * seen[q]) * r
-            d = jnp.where(sub == k, pivot, d)
-            e = jnp.where(sub == k, r, e)
-            m = jnp.where(sub > k, cols[k] * r, 0.0)
-            a_rows.append(row_of(a[s], k))
-            a[s] = a[s] - m * a_rows[k]
+        near = [column_of(a[s + 1], 8 * s + k) for k in range(8)] if s + 1 < tiles else None
+        d, e = zero, zero
+        for k in range(0, 8, 2):
+            first, second = cols[k], cols[k + 1]
+            p, q, t = row_of(first, k), row_of(first, k + 1), row_of(second, k + 1)
+            rd = reciprocal(p * t - q * q)
+            rp = reciprocal(p)
+            weights = {}
+            for n in range(k + 2, 8):
+                x, y = row_of(cols[n], k), row_of(cols[n], k + 1)
+                weights[n] = (t * x - q * y) * rd, (p * y - q * x) * rd
+                cols[n] = cols[n] - first * weights[n][0] - second * weights[n][1]
+            qp = q * rp
+            r1 = p * rd
+            d = jnp.where(sub == k, p, jnp.where(sub == k + 1, t - q * qp, d))
+            e = jnp.where(sub == k, rp, jnp.where(sub == k + 1, r1, e))
+            m0 = jnp.where(sub > k, first * rp, 0.0)
+            m1 = jnp.where(sub > k + 1, (second - first * qp) * r1, 0.0)
+            a0 = row_of(a[s], k)
+            a[s] = a[s] - m0 * a0
+            a1 = row_of(a[s], k + 1)
+            a[s] = a[s] - m1 * a1
             if b is not None:
-                b_rows.append(row_of(b[s], k))
-                b[s] = b[s] - m * b_rows[k]
-            inv.append(r)
-            known.append(seen)
+                b0 = row_of(b[s], k)
+                b[s] = b[s] - m0 * b0
+                b1 = row_of(b[s], k + 1)
+                b[s] = b[s] - m1 * b1
+            if near is not None:
+                n0 = near[k] * rp
+                n1 = (near[k + 1] - near[k] * qp) * r1
+                for n in range(k + 2, 8):
+                    near[n] = near[n] - near[k] * weights[n][0] - near[k + 1] * weights[n][1]
+                a[s + 1] = a[s + 1] - n0 * a0 - n1 * a1
+                if b is not None:
+                    b[s + 1] = b[s + 1] - n0 * b0 - n1 * b1
         diag.append(d)
         if s + 2 < tiles:
-            turned = jnp.transpose(a[s] * e)
-        for i in range(s + 1, tiles):
-            if i == s + 1:
-                cols = [column_of(a[i], 8 * s + k) for k in range(8)]
-            for k in range(8):
-                if i == s + 1:
-                    m = cols[k] * inv[k]
-                    for q in range(k + 1, 8):
-                        cols[q] = cols[q] - m * known[k][q]
-                else:
-                    m = column_of(turned[8 * i : 8 * i + 8, :], k)
-                a[i] = a[i] - m * a_rows[k]
+            vh, vl = parts_of(a[s] * e)
+            wide = a[s] if b is None else jnp.concatenate([a[s], b[s]], axis=1)
+            uh, ul = parts_of(wide)
+            delta = lax.dot_general(
+                jnp.concatenate([vh, vh, vl, zero], axis=0).astype(BF16),
+                jnp.concatenate([uh, ul, uh, jnp.zeros_like(uh)], axis=0).astype(BF16),
+                TN, preferred_element_type=F32,
+            )
+            for i in range(s + 2, tiles):
+                a[i] = a[i] - delta[8 * i : 8 * i + 8, :128]
                 if b is not None:
-                    b[i] = b[i] - m * b_rows[k]
+                    b[i] = b[i] - delta[8 * i : 8 * i + 8, 128:]
     scale = []
     for d in diag:
         y = lax.rsqrt(d)
@@ -345,7 +363,7 @@
     return hi, (x - hi.astype(F32)).astype(BF16)
 
 
-def factor_kernel(count, n_feat, all_ref, s1_ref, s2_ref, c_ref, o_ref, fa_ref, fb_ref, a_ref, u_ref, l_ref):
+def factor_kernel(count, n_feat, all_ref, s1_ref, s2_ref, c_ref, o_ref, f_ref, fa_ref, fb_ref, a_ref, u_ref, l_ref):
     n_tm, chunks = all_ref.shape[:2]
     padded = s1_ref.shape[0]
     blocks = padded // 128
@@ -368,6 +386,7 @@
     lane = lax.broadcasted_iota(jnp.int32, (modes, lanes), 1)
     top = lax.broadcasted_iota(jnp.int32, (modes, lanes), 0)
     ones = jnp.where(jnp.logical_and(lane < count, top == 0), 1.0, 0.0).astype(BF16)
+    squares = jnp.zeros((padded, 1), F32)
     for g in range(n_tm):
         c = coeffs(g)
         hi = c.astype(BF16)
@@ -377,7 +396,15 @@
         stack = jnp.concatenate([hi, mid, low, ones], axis=0)
         f1 = jnp.dot(s1_ref[...], stack, preferred_element_type=F32)
         f2 = jnp.dot(s2_ref[...], stack, preferred_element_type=F32)
-        fh, fl = split(f1 * f2)
+        f = f1 * f2
+        f_ref[:, pl.ds(g * lanes, lanes)] = f
+        squares = squares + jnp.sum(f * f, axis=1, keepdims=True)
+    inverse = jnp.where(squares > 0.0, lax.rsqrt(squares), 0.0)
+    inverse = inverse * (1.5 - 0.5 * squares * inverse * inverse)
+    size = squares * inverse * (1.0 / np.sqrt(count * n_tm))
+    sizes = jnp.transpose(jnp.broadcast_to(size, (padded, 128)))[0:8, :]
+    for g in range(n_tm):
+        fh, fl = split(f_ref[:, pl.ds(g * lanes, lanes)] * inverse)
         at = [pl.ds((part * n_tm + g) * lanes, lanes) for part in range(3)]
         fa_ref[:, at[0]] = fh
         fa_ref[:, at[1]] = fh
@@ -386,13 +413,12 @@
         fb_ref[:, at[1]] = fl
         fb_ref[:, at[2]] = fh
 
-    share_of = 1.0 / (count * n_tm)
     for j in range(blocks):
         gram = lax.dot_general(
             fa_ref[pl.ds(j * 128, 128), :], fb_ref[pl.ds(j * 128, padded - j * 128), :], NT,
             preferred_element_type=F32,
         )
-        a_ref[pl.ds(j * 128, 128), pl.ds(j * 128, padded - j * 128)] = gram * share_of
+        a_ref[pl.ds(j * 128, 128), pl.ds(j * 128, padded - j * 128)] = gram
 
     last = (blocks - 1) * 128
     ri = lax.broadcasted_iota(jnp.int32, (128, 128), 0)
@@ -420,7 +446,7 @@
                 here, after = jj * 128, (jj + 1) * 128
                 if jj > 0:
                     o_ref[pl.ds(here, 128), pl.ds(0, here)] = jnp.zeros((128, here), F32)
-                o_ref[pl.ds(here, 128), pl.ds(here, 128)] = u_ref[...]
+                o_ref[pl.ds(here, 128), pl.ds(here, 128)] = u_ref[...] * sizes[0:1, here:after]
                 lh, ll = split(l_ref[...])
                 ah, al = split(a_ref[pl.ds(here, 128), pl.ds(after, padded - after)])
                 w = jnp.dot(
@@ -429,7 +455,9 @@
                 )
                 wh, wl = split(w)
                 left, right = jnp.concatenate([wh, wh, wl], axis=0), jnp.concatenate([wh, wl, wh], axis=0)
-                o_ref[pl.ds(here, 128), pl.ds(after, n_feat - after)] = w[:, : n_feat - after]
+                o_ref[pl.ds(here, 128), pl.ds(after, n_feat - after)] = (
+                    w[:, : n_feat - after] * sizes[0:1, after:n_feat]
+                )
                 for i in range(jj + 1, blocks):
                     row = i * 128
                     a_ref[pl.ds(row, 128), pl.ds(row, padded - row)] -= lax.dot_general(
@@ -446,7 +474,7 @@
     for i in range(tiles):
         u_ref[pl.ds(8 * i, 8), :] = jnp.where(lane8 >= sub8 + 8 * i, a[i] * scale[i], 0.0)
     o_ref[pl.ds(last, left), pl.ds(0, last)] = jnp.zeros((left, last), F32)
-    o_ref[pl.ds(last, left), pl.ds(last, left)] = u_ref[pl.ds(0, left), pl.ds(0, left)]
+    o_ref[pl.ds(last, left), pl.ds(last, left)] = u_ref[pl.ds(0, left), pl.ds(0, left)] * sizes[0:1, last:n_feat]
 
 
 def selections(modes):
@@ -480,13 +508,14 @@
         in_specs=[vmem] * 3,
         out_specs=(vmem, vmem),
         scratch_shapes=[
+            pltpu.VMEM((padded, n_tm * lanes), F32),
             pltpu.VMEM((padded, 3 * n_tm * lanes), BF16),
             pltpu.VMEM((padded, 3 * n_tm * lanes), BF16),
             pltpu.VMEM((padded, padded), F32),
             pltpu.VMEM((128, 128), F32),
             pltpu.VMEM((128, 128), F32),
         ],
-        compiler_params=pltpu.CompilerParams(vmem_limit_bytes=48 * 2**20),
+        compiler_params=pltpu.CompilerParams(vmem_limit_bytes=60 * 2**20),
         name="factorize",
     )(shared, jnp.asarray(s1, BF16), jnp.asarray(s2, BF16))
 

time: 68.6 us -> 60 us (0.87)
  local copies, waits for them, and re-layouts: 5.01 us -> 0 us
  Pallas kernels: 62.6 us -> 59.2 us
    unnamed x12 -> x0, local copies, waits for them, and re-layouts: 5.01 us -> none
    pallas_call x1, Pallas kernels: 29.7 us -> 25.9 us  [factorize(): pl.pallas_call(functools.partial(factor_kernel, count, n_feat), out_shape...]
where the time goes in v3:
time: 60 us; the launch traced here: 59.9 us
  Pallas kernels  59.2 us (99%)
  between operations  0.64 us (1%)
    pallas_call x1, Pallas kernels, gather_coefficients(): pl.pallas_call(functools.partial(gather_kernel, n_tm, n_space, chunks), o...  33.4 us
    pallas_call x1, Pallas kernels, factorize(): pl.pallas_call(functools.partial(factor_kernel, count, n_feat), out_shape...  25.9 us

profile of v3, /device:TPU:0, one launch (start us, length us, event | category | flops | bytes accessed | tf_op | source)
XLA Modules:
  0.0 59.9 jit_solution(11097525202731065254)
XLA Ops:
  0.6 33.4 %gather_coefficients.1.all_ref = f32[4,8,8,128]{3,2,1,0:T(8,128)} custom-call(bf16[252,5,2,8,128]{4,3,2,1,0:T(8,128)(2,1)} %s_any.1, bf16[32,5,2,8,128]{4,3,2,1,0:T(8,128)(2,1)} %b_any.1, f32[5,2,8,128]{3,2,1,0:T(8,128)} %k_any.1, s32[1,224]{1,0:T(1,128)} %bitcast.2), custom_call_target="tpu_custom_call" | custom-call | tf_op jit(solution)/shard_map/gather_coefficients/pallas_call | solution.py:261
  34.0 25.9 %factorize.1 = (f32[32,224]{1,0:T(8,128)}, f32[561,561]{1,0:T(8,128)}) custom-call(f32[4,8,8,128]{3,2,1,0:T(8,128)} %gather_coefficients.1.all_ref, bf16[640,128]{1,0:T(8,128)(2,1)} %constant.4.clone.s1_ref, bf16[640,128]{1,0:T(8,128)(2,1)} %constant.5.clone.s2_ref), custom_call_target="tpu_custom_call" | custom-call | tf_op jit(solution)/shard_map/factorize/pallas_call | solution.py:502

commit v4 on v3

--- a/solution.py
+++ b/solution.py
@@ -17,10 +17,17 @@
 BF16 = jnp.bfloat16
 
 
+def thirds(x):
+    hi = x.astype(BF16)
+    rest = x - hi.astype(F32)
+    mid = rest.astype(BF16)
+    return hi, mid, (rest - mid.astype(F32)).astype(BF16)
+
+
 def gather_kernel(
     n_tm, n_space, chunks, s_any, b_any, k_any, picks_ref, all_ref,
     s_ref, b_ref, k_ref, g_ref, z_ref, hb_ref, hk_ref, own_ref, land_ref,
-    load, load_b, load_k, send_b, recv_b, send_k, recv_k, send_f, recv_f, send1, recv1, send2, recv2,
+    load, load_b, load_k, send_b, recv_b, send_k, recv_k, send_f, recv_f, send1, recv1, send2, recv2, send3, recv3,
 ):
     count, nv, nx, ny, nz = s_any.shape
     modes = b_any.shape[0]
@@ -31,12 +38,13 @@
     sp = lax.axis_index("space")
     core = lax.rem(tm, 2)
     sibling = tm + 1 - 2 * core
-    me = tm * n_space + sp
-    total = n_tm * n_space
+    column = lax.div(tm, 2)
+    me = column * n_space + sp
+    total = (n_tm // 2) * n_space
 
     def peer(i):
         other = lax.rem(me + i, total)
-        return other // n_space, lax.rem(other, n_space)
+        return 2 * lax.div(other, n_space) + core, lax.rem(other, n_space)
 
     loading_b = pltpu.make_async_copy(b_any, b_ref, load_b)
     loading_k = pltpu.make_async_copy(k_any, k_ref, load_k)
@@ -51,7 +59,8 @@
         return carry
 
     lax.fori_loop(1, total, greet, 0)
-    pl.semaphore_wait(barrier, total - 1)
+    pl.semaphore_signal(barrier, inc=1, device_id=(sibling, sp), device_id_type=MESH)
+    pl.semaphore_wait(barrier, total)
 
     def remote(src, dst, send, recv, device):
         return pltpu.make_async_remote_copy(
@@ -170,13 +179,19 @@
     fold = (
         lax.broadcasted_iota(jnp.int32, (modes, wide), 1) // ny
         == lax.broadcasted_iota(jnp.int32, (modes, wide), 0)
-    ).astype(F32)
-    part = lax.dot_general(fold, z_ref[...], NT, precision=HIGHEST, preferred_element_type=F32)
+    ).astype(BF16)
+    part = lax.dot_general(
+        jnp.concatenate([fold] * 3, axis=1), jnp.concatenate(thirds(z_ref[...]), axis=1), NT,
+        preferred_element_type=F32,
+    )
     hot = (
         lax.broadcasted_iota(jnp.int32, (rows_all, taken), 0)
         == jnp.broadcast_to(picks_ref[...], (rows_all, taken))
-    ).astype(F32)
-    mine = jnp.dot(part, hot, precision=HIGHEST, preferred_element_type=F32)
+    ).astype(BF16)
+    mine = jnp.dot(
+        jnp.concatenate(thirds(part), axis=1), jnp.concatenate([hot] * 3, axis=0),
+        preferred_element_type=F32,
+    )
     halves = -(-taken // 128)
     for i in range(modes // 8):
         for h in range(halves):
@@ -195,8 +210,12 @@
 
     def give_to(i):
         return remote(
-            all_ref.at[tm, sp], all_ref.at[tm, sp], send2.at[i], recv2.at[tm * chunks + sp], peer(i)
-        )
+            all_ref.at[core, column, sp], all_ref.at[core, column, sp],
+            send2.at[i], recv2.at[column * chunks + sp], peer(i),
+        )
+
+    def hand_over(which):
+        return remote(all_ref.at[which], all_ref.at[which], send3, recv3, (sibling, sp))
 
     @pl.when(sp < chunks)
     def _():
@@ -210,7 +229,7 @@
         total_sum = land_ref[0]
         for source in range(1, n_space):
             total_sum = total_sum + land_ref[source]
-        all_ref[tm, sp] = total_sum
+        all_ref[core, column, sp] = total_sum
 
         def give(i, carry):
             give_to(i).start()
@@ -218,6 +237,17 @@
 
         lax.fori_loop(1, total, give, 0)
 
+    for group in range(n_tm // 2):
+        for owner in range(chunks):
+            @pl.when(jnp.logical_or(column != group, sp != owner))
+            def _():
+                remote(
+                    all_ref.at[core, group, owner], all_ref.at[core, group, owner],
+                    send2.at[0], recv2.at[group * chunks + owner], (2 * group + core, owner),
+                ).wait_recv()
+
+    hand_over(core).start()
+
     for side in range(2):
         @pl.when(sends[side])
         def _():
@@ -232,15 +262,6 @@
         @pl.when(sp != owner)
         def _():
             part_to(owner).wait_send()
-
-    for group in range(n_tm):
-        for owner in range(chunks):
-            @pl.when(jnp.logical_or(tm != group, sp != owner))
-            def _():
-                remote(
-                    all_ref.at[group, owner], all_ref.at[group, owner],
-                    send2.at[0], recv2.at[group * chunks + owner], (group, owner),
-                ).wait_recv()
 
     @pl.when(sp < chunks)
     def _():
@@ -249,6 +270,9 @@
             return carry
 
         lax.fori_loop(1, total, done, 0)
+
+    hand_over(core).wait_send()
+    hand_over(1 - core).wait_recv()
 
 
 def gather_coefficients(snapshots, basis, kappa, picks_row, n_tm, n_space):
@@ -260,7 +284,7 @@
     dma = pltpu.SemaphoreType.DMA
     return pl.pallas_call(
         functools.partial(gather_kernel, n_tm, n_space, chunks),
-        out_shape=jax.ShapeDtypeStruct((n_tm, chunks, 8, 128), F32),
+        out_shape=jax.ShapeDtypeStruct((2, n_tm // 2, chunks, 8, 128), F32),
         in_specs=[pl.BlockSpec(memory_space=pltpu.HBM)] * 3 + [vmem],
         out_specs=vmem,
         scratch_shapes=[
@@ -274,7 +298,8 @@
             pltpu.VMEM((chunks, 8, 128), F32),
             pltpu.VMEM((n_space, 8, 128), F32),
             dma, dma, dma, dma((2,)), dma((2,)), dma((2,)), dma((2,)), dma((2,)), dma((2,)),
-            dma((chunks,)), dma((n_space,)), dma((n_tm * n_space,)), dma((n_tm * chunks,)),
+            dma((chunks,)), dma((n_space,)), dma((n_tm // 2 * n_space,)), dma((n_tm // 2 * chunks,)),
+            dma, dma,
         ],
         compiler_params=pltpu.CompilerParams(
             collective_id=0, has_side_effects=True, vmem_limit_bytes=60 * 2**20
@@ -364,7 +389,7 @@
 
 
 def factor_kernel(count, n_feat, all_ref, s1_ref, s2_ref, c_ref, o_ref, f_ref, fa_ref, fb_ref, a_ref, u_ref, l_ref):
-    n_tm, chunks = all_ref.shape[:2]
+    n_tm, chunks = 2 * all_ref.shape[1], all_ref.shape[2]
     padded = s1_ref.shape[0]
     blocks = padded // 128
     halves = -(-count // 128)
@@ -373,27 +398,23 @@
     modes = 8 * groups
     tm = lax.axis_index("tm")
 
-    def coeffs(g):
+    def coeffs(core, column):
         return jnp.concatenate(
             [
-                jnp.concatenate([all_ref[g, i * halves + h] for h in range(halves)], axis=1)
+                jnp.concatenate([all_ref[core, column, i * halves + h] for h in range(halves)], axis=1)
                 for i in range(groups)
             ],
             axis=0,
         )
 
-    c_ref[...] = coeffs(tm)[:, :count]
+    c_ref[...] = coeffs(lax.rem(tm, 2), lax.div(tm, 2))[:, :count]
     lane = lax.broadcasted_iota(jnp.int32, (modes, lanes), 1)
     top = lax.broadcasted_iota(jnp.int32, (modes, lanes), 0)
     ones = jnp.where(jnp.logical_and(lane < count, top == 0), 1.0, 0.0).astype(BF16)
     squares = jnp.zeros((padded, 1), F32)
     for g in range(n_tm):
-        c = coeffs(g)
-        hi = c.astype(BF16)
-        rest = c - hi.astype(F32)
-        mid = rest.astype(BF16)
-        low = (rest - mid.astype(F32)).astype(BF16)
-        stack = jnp.concatenate([hi, mid, low, ones], axis=0)
+        c = coeffs(g % 2, g // 2)
+        stack = jnp.concatenate([*thirds(c), ones], axis=0)
         f1 = jnp.dot(s1_ref[...], stack, preferred_element_type=F32)
         f2 = jnp.dot(s2_ref[...], stack, preferred_element_type=F32)
         f = f1 * f2
@@ -413,12 +434,12 @@
         fb_ref[:, at[1]] = fl
         fb_ref[:, at[2]] = fh
 
-    for j in range(blocks):
-        gram = lax.dot_general(
-            fa_ref[pl.ds(j * 128, 128), :], fb_ref[pl.ds(j * 128, padded - j * 128), :], NT,
+    for col in range(0, padded, 256):
+        end = min(col + 256, padded)
+        a_ref[pl.ds(0, end), pl.ds(col, end - col)] = lax.dot_general(
+            fa_ref[pl.ds(0, end), :], fb_ref[pl.ds(col, end - col), :], NT,
             preferred_element_type=F32,
         )
-        a_ref[pl.ds(j * 128, 128), pl.ds(j * 128, padded - j * 128)] = gram
 
     last = (blocks - 1) * 128
     ri = lax.broadcasted_iota(jnp.int32, (128, 128), 0)
@@ -458,10 +479,10 @@
                 o_ref[pl.ds(here, 128), pl.ds(after, n_feat - after)] = (
                     w[:, : n_feat - after] * sizes[0:1, after:n_feat]
                 )
-                for i in range(jj + 1, blocks):
-                    row = i * 128
-                    a_ref[pl.ds(row, 128), pl.ds(row, padded - row)] -= lax.dot_general(
-                        left[:, row - after : row - after + 128], right[:, row - after :], TN,
+                for col in range(after, padded, 256):
+                    end = min(col + 256, padded)
+                    a_ref[pl.ds(after, end - after), pl.ds(col, end - col)] -= lax.dot_general(
+                        left[:, : end - after], right[:, col - after : end - after], TN,
                         preferred_element_type=F32,
                     )
         return carry
@@ -495,7 +516,7 @@
 
 
 def factorize(shared, count, modes):
-    n_tm = shared.shape[0]
+    n_tm = 2 * shared.shape[1]
     n_feat, padded, s1, s2 = selections(modes)
     lanes = -(-count // 128) * 128
     vmem = pl.BlockSpec(memory_space=pltpu.VMEM)

time: 60 us -> 58.8 us (0.980)
  Pallas kernels: 59.2 us -> 58 us
    pallas_call x1, Pallas kernels: 33.4 us -> 32.3 us  [gather_coefficients(): pl.pallas_call(functools.partial(gather_kernel, n_tm, n_space, chunks), o...]
where the time goes in v4:
time: 58.8 us; the launch traced here: 58.6 us
  Pallas kernels  58 us (99%)
  between operations  0.64 us (1%)
    pallas_call x1, Pallas kernels, gather_coefficients(): pl.pallas_call(functools.partial(gather_kernel, n_tm, n_space, chunks), o...  32.3 us
    pallas_call x1, Pallas kernels, factorize(): pl.pallas_call(functools.partial(factor_kernel, count, n_feat), out_shape...  25.7 us

profile of v4, /device:TPU:0, one launch (start us, length us, event | category | flops | bytes accessed | tf_op | source)
XLA Modules:
  0.0 58.6 jit_solution(9402462765254786519)
XLA Ops:
  0.6 32.3 %gather_coefficients.1.all_ref = f32[2,2,8,8,128]{4,3,2,1,0:T(8,128)} custom-call(bf16[252,5,2,8,128]{4,3,2,1,0:T(8,128)(2,1)} %s_any.1, bf16[32,5,2,8,128]{4,3,2,1,0:T(8,128)(2,1)} %b_any.1, f32[5,2,8,128]{3,2,1,0:T(8,128)} %k_any.1, s32[1,224]{1,0:T(1,128)} %bitcast.2), custom_call_target="tpu_custom_call" | custom-call | tf_op jit(solution)/shard_map/gather_coefficients/pallas_call | solution.py:285
  32.9 25.7 %factorize.1 = (f32[32,224]{1,0:T(8,128)}, f32[561,561]{1,0:T(8,128)}) custom-call(f32[2,2,8,8,128]{4,3,2,1,0:T(8,128)} %gather_coefficients.1.all_ref, bf16[640,128]{1,0:T(8,128)(2,1)} %constant.4.clone.s1_ref, bf16[640,128]{1,0:T(8,128)(2,1)} %constant.5.clone.s2_ref), custom_call_target="tpu_custom_call" | custom-call | tf_op jit(solution)/shard_map/factorize/pallas_call | solution.py:523

commit v5 on v4

--- a/solution.py
+++ b/solution.py
@@ -26,7 +26,7 @@
 
 def gather_kernel(
     n_tm, n_space, chunks, s_any, b_any, k_any, picks_ref, all_ref,
-    s_ref, b_ref, k_ref, g_ref, z_ref, hb_ref, hk_ref, own_ref, land_ref,
+    s_ref, rows_ref, b_ref, k_ref, g_ref, z_ref, hb_ref, hk_ref, own_ref, land_ref,
     load, load_b, load_k, send_b, recv_b, send_k, recv_k, send_f, recv_f, send1, recv1, send2, recv2, send3, recv3,
 ):
     count, nv, nx, ny, nz = s_any.shape
@@ -134,17 +134,21 @@
     yr = lax.broadcasted_iota(jnp.int32, (CHUNK * ny, wide), 0) % ny
     yc = lax.broadcasted_iota(jnp.int32, (CHUNK * ny, wide), 1) % ny
 
-    def contract(i):
+    def lay(i):
         at = pl.ds(i * CHUNK, CHUNK)
-        rows = jnp.concatenate(
+        return jnp.concatenate(
             [s_ref[at, v, x].reshape(CHUNK * ny, nz) for v in range(nv) for x in range(nx)], axis=1
         )
+
+    def contract(rows):
         both = lax.dot_general(rows, g_ref[...], NT, preferred_element_type=F32)
         prod = both[:, :wide] + both[:, wide:]
         return jnp.sum(jnp.where(yr == yc, prod, 0.0).reshape(CHUNK, ny, wide), axis=1)
 
     def inner(i, carry):
-        z_ref[pl.ds(pl.multiple_of(i * CHUNK, CHUNK), CHUNK), :] = contract(i)
+        rows = lay(i)
+        rows_ref[pl.ds(pl.multiple_of(i * CHUNK * ny, CHUNK * ny), CHUNK * ny), :] = rows
+        z_ref[pl.ds(pl.multiple_of(i * CHUNK, CHUNK), CHUNK), :] = contract(rows)
         return carry
 
     lax.fori_loop(0, rows_all // CHUNK, inner, 0)
@@ -171,7 +175,8 @@
     outer_modes(1 - core)
 
     def outer(i, carry):
-        z_ref[pl.ds(pl.multiple_of(i * CHUNK, CHUNK), CHUNK), :] += contract(i)
+        rows = rows_ref[pl.ds(pl.multiple_of(i * CHUNK * ny, CHUNK * ny), CHUNK * ny), :]
+        z_ref[pl.ds(pl.multiple_of(i * CHUNK, CHUNK), CHUNK), :] += contract(rows)
         return carry
 
     lax.fori_loop(0, rows_all // CHUNK, outer, 0)
@@ -289,6 +294,7 @@
         out_specs=vmem,
         scratch_shapes=[
             pltpu.VMEM((rows_all, nv, nx, ny, nz), BF16),
+            pltpu.VMEM((rows_all * ny, nv * nx * nz), BF16),
             pltpu.VMEM(basis.shape, BF16),
             pltpu.VMEM(kappa.shape, F32),
             pltpu.VMEM((2 * modes * ny, nv * nx * nz), BF16),
@@ -388,7 +394,7 @@
     return hi, (x - hi.astype(F32)).astype(BF16)
 
 
-def factor_kernel(count, n_feat, all_ref, s1_ref, s2_ref, c_ref, o_ref, f_ref, fa_ref, fb_ref, a_ref, u_ref, l_ref):
+def factor_kernel(count, n_feat, all_ref, s1_ref, s2_ref, c_ref, o_ref, f_ref, fa_ref, fb_ref, a_ref, u_ref):
     n_tm, chunks = 2 * all_ref.shape[1], all_ref.shape[2]
     padded = s1_ref.shape[0]
     blocks = padded // 128
@@ -452,42 +458,46 @@
     lane8 = lax.broadcasted_iota(jnp.int32, (8, 128), 1)
     sub8 = lax.broadcasted_iota(jnp.int32, (8, 128), 0)
 
-    def block(j, carry):
-        start = pl.multiple_of(j * 128, 128)
-        a = [a_ref[pl.ds(start + 8 * i, 8), pl.ds(start, 128)] for i in range(16)]
+    for j in range(blocks - 1):
+        here, after = j * 128, (j + 1) * 128
+        a = [a_ref[pl.ds(here + 8 * i, 8), pl.ds(here, 128)] for i in range(16)]
         b = [jnp.where(lane8 == sub8 + 8 * i, 1.0, 0.0) for i in range(16)]
         a, b, scale = eliminate(a, b)
+        lh, ll = split(jnp.concatenate([b[i] * scale[i] for i in range(16)], axis=0))
+        inverse_rows = jnp.concatenate([lh, lh, ll], axis=1)
+
+        def solve(col, end):
+            ah, al = split(a_ref[pl.ds(here, 128), pl.ds(col, end - col)])
+            w = jnp.dot(
+                inverse_rows, jnp.concatenate([ah, al, ah], axis=0), preferred_element_type=F32
+            )
+            stop = min(end, n_feat)
+            o_ref[pl.ds(here, 128), pl.ds(col, stop - col)] = w[:, : stop - col] * sizes[0:1, col:stop]
+            wh, wl = split(w)
+            return jnp.concatenate([wh, wh, wl], axis=0), jnp.concatenate([wh, wl, wh], axis=0)
+
+        def update(lhs, rhs, row, col):
+            at = pl.ds(row, lhs.shape[1]), pl.ds(col, rhs.shape[1])
+            a_ref[at] -= lax.dot_general(lhs, rhs, TN, preferred_element_type=F32)
+
+        left, right = solve(after, after + 128)
+        update(left, right, after, after)
+        rest = after + 128
+        if rest < padded:
+            more_left, more_right = solve(rest, padded)
+            for col in range(rest, padded, 256):
+                end = min(col + 256, padded)
+                update(
+                    jnp.concatenate([left, more_left[:, : end - rest]], axis=1),
+                    more_right[:, col - rest : end - rest], after, col,
+                )
         for i in range(16):
-            u_ref[pl.ds(8 * i, 8), :] = jnp.where(lane8 >= sub8 + 8 * i, a[i] * scale[i], 0.0)
-            l_ref[pl.ds(8 * i, 8), :] = b[i] * scale[i]
-
-        for jj in range(blocks - 1):
-            @pl.when(j == jj)
-            def _():
-                here, after = jj * 128, (jj + 1) * 128
-                if jj > 0:
-                    o_ref[pl.ds(here, 128), pl.ds(0, here)] = jnp.zeros((128, here), F32)
-                o_ref[pl.ds(here, 128), pl.ds(here, 128)] = u_ref[...] * sizes[0:1, here:after]
-                lh, ll = split(l_ref[...])
-                ah, al = split(a_ref[pl.ds(here, 128), pl.ds(after, padded - after)])
-                w = jnp.dot(
-                    jnp.concatenate([lh, lh, ll], axis=1), jnp.concatenate([ah, al, ah], axis=0),
-                    preferred_element_type=F32,
-                )
-                wh, wl = split(w)
-                left, right = jnp.concatenate([wh, wh, wl], axis=0), jnp.concatenate([wh, wl, wh], axis=0)
-                o_ref[pl.ds(here, 128), pl.ds(after, n_feat - after)] = (
-                    w[:, : n_feat - after] * sizes[0:1, after:n_feat]
-                )
-                for col in range(after, padded, 256):
-                    end = min(col + 256, padded)
-                    a_ref[pl.ds(after, end - after), pl.ds(col, end - col)] -= lax.dot_general(
-                        left[:, : end - after], right[:, col - after : end - after], TN,
-                        preferred_element_type=F32,
-                    )
-        return carry
-
-    lax.fori_loop(0, blocks - 1, block, 0)
+            o_ref[pl.ds(here + 8 * i, 8), pl.ds(here, 128)] = (
+                jnp.where(lane8 >= sub8 + 8 * i, a[i] * scale[i], 0.0) * sizes[0:1, here:after]
+            )
+        if j > 0:
+            o_ref[pl.ds(here, 128), pl.ds(0, here)] = jnp.zeros((128, here), F32)
+
     left = n_feat - last
     tiles = -(-left // 8)
     a = [a_ref[pl.ds(last + 8 * i, 8), pl.ds(last, 128)] for i in range(tiles)]
@@ -534,7 +544,6 @@
             pltpu.VMEM((padded, 3 * n_tm * lanes), BF16),
             pltpu.VMEM((padded, padded), F32),
             pltpu.VMEM((128, 128), F32),
-            pltpu.VMEM((128, 128), F32),
         ],
         compiler_params=pltpu.CompilerParams(vmem_limit_bytes=60 * 2**20),
         name="factorize",

time: 58.8 us -> 56.3 us (0.957)
  Pallas kernels: 58 us -> 55.5 us
    pallas_call x1, Pallas kernels: 25.7 us -> 23.2 us  [factorize(): pl.pallas_call(functools.partial(factor_kernel, count, n_feat), out_shape...]
where the time goes in v5:
time: 56.3 us; the launch traced here: 56.1 us
  Pallas kernels  55.5 us (99%)
  between operations  0.64 us (1%)
    pallas_call x1, Pallas kernels, gather_coefficients(): pl.pallas_call(functools.partial(gather_kernel, n_tm, n_space, chunks), o...  32.3 us
    pallas_call x1, Pallas kernels, factorize(): pl.pallas_call(functools.partial(factor_kernel, count, n_feat), out_shape...  23.2 us

profile of v5, /device:TPU:0, one launch (start us, length us, event | category | flops | bytes accessed | tf_op | source)
XLA Modules:
  0.0 56.1 jit_solution(756831050022369674)
XLA Ops:
  0.6 32.3 %gather_coefficients.1.all_ref = f32[2,2,8,8,128]{4,3,2,1,0:T(8,128)} custom-call(bf16[252,5,2,8,128]{4,3,2,1,0:T(8,128)(2,1)} %s_any.1, bf16[32,5,2,8,128]{4,3,2,1,0:T(8,128)(2,1)} %b_any.1, f32[5,2,8,128]{3,2,1,0:T(8,128)} %k_any.1, s32[1,224]{1,0:T(1,128)} %bitcast.2), custom_call_target="tpu_custom_call" | custom-call | tf_op jit(solution)/shard_map/gather_coefficients/pallas_call | solution.py:290
  32.9 23.2 %factorize.1 = (f32[32,224]{1,0:T(8,128)}, f32[561,561]{1,0:T(8,128)}) custom-call(f32[2,2,8,8,128]{4,3,2,1,0:T(8,128)} %gather_coefficients.1.all_ref, bf16[640,128]{1,0:T(8,128)(2,1)} %constant.4.clone.s1_ref, bf16[640,128]{1,0:T(8,128)(2,1)} %constant.5.clone.s2_ref), custom_call_target="tpu_custom_call" | custom-call | tf_op jit(solution)/shard_map/factorize/pallas_call | solution.py:533
